TPU v7x, 256 devices: a whole 4x4x8 slice. The times are simulated.
256 devices in a mesh: ctx: 64 (over z, y, x_lo), head: 4 (over x_hi, core).
Axes of the slice: x: 4 (x_hi: 2, x_lo: 2; x = x_hi * 2 + x_lo), y: 4, z: 8, core: 2. Of those that a mesh axis runs over, the one named last changes fastest.
Arguments:
- queries: bfloat16 [32768, 4096], P(('ctx', 'head')), may hold values from -6 to 6
- keys: bfloat16 [32768, 1024], P(('ctx', 'head')), may hold values from -6 to 6
- values: bfloat16 [32768, 1024], P(('ctx', 'head')), may hold values from -6 to 6
- cotangent: bfloat16 [32768, 4096], P(('ctx', 'head')), may hold values from -6 to 6
Outputs:
- out: bfloat16 [32768, 4096], P(('ctx', 'head'))
- grad_queries: bfloat16 [32768, 4096], P(('ctx', 'head'))
- grad_keys: bfloat16 [32768, 1024], P(('ctx', 'head'))
- grad_values: bfloat16 [32768, 1024], P(('ctx', 'head'))
All inputs are finite; a program needn't handle non-finite values.
Results may differ from a plain program's by a relative error of at most 0.008.
Values may be sent and summed in bfloat16 or wider, within the bound.
A program may use at most 64 MiB of HBM per device.

v0:
```python
import jax
import jax.numpy as jnp
from jax import lax
from jax.sharding import PartitionSpec as P

QUERY_HEADS = 32
KEY_VALUE_HEADS = 8
HEAD_FEATURES = 128
BLOCK_POSITIONS = 512


LOWEST = -1e30


def from_behind(block, axis, distance):
    devices = range(lax.axis_size(axis))
    route = [(i - distance, i) for i in devices if i - distance in devices]
    return lax.ppermute(block, axis, route)


def head_terms(
    query, grad_out, band_keys, band_values, block_summary_keys, block_summary_values, first, keep
):
    row_count = query.shape[0]
    width = band_keys.shape[0]
    scale = query.shape[1] ** (-0.5)
    query_pos = first + jnp.arange(row_count, dtype=jnp.int32)
    key_pos = first - (width - row_count) + jnp.arange(width, dtype=jnp.int32)
    band_mask = (key_pos[None, :] >= 0) & (key_pos[None, :] <= query_pos[:, None])
    summary_mask = (
        jnp.arange(block_summary_keys.shape[0], dtype=jnp.int32)[None, :] < first // BLOCK_POSITIONS
    )
    band_score = jnp.dot(query, band_keys.T, preferred_element_type=jnp.float32) * scale
    summary_score = jnp.dot(query, block_summary_keys.T, preferred_element_type=jnp.float32) * scale
    row_top = jnp.maximum(
        jnp.max(jnp.where(band_mask, band_score, LOWEST), axis=1),
        jnp.max(jnp.where(summary_mask, summary_score, LOWEST), axis=1),
    )
    band_weight = jnp.where(band_mask, jnp.exp(band_score - row_top[:, None]), 0.0)
    summary_weight = jnp.where(summary_mask, jnp.exp(summary_score - row_top[:, None]), 0.0)
    row_total = jnp.sum(band_weight, axis=1) + jnp.sum(summary_weight, axis=1)
    band_prob = band_weight / row_total[:, None]
    summary_prob = summary_weight / row_total[:, None]
    band_low = band_prob.astype(jnp.bfloat16)
    summary_low = summary_prob.astype(jnp.bfloat16)
    attended = jnp.dot(band_low, band_values, preferred_element_type=jnp.float32) + jnp.dot(
        summary_low, block_summary_values, preferred_element_type=jnp.float32
    )
    row_dot = jnp.sum(grad_out.astype(jnp.float32) * attended, axis=1)
    band_back = jnp.dot(grad_out, band_values.T, preferred_element_type=jnp.float32)
    summary_back = jnp.dot(grad_out, block_summary_values.T, preferred_element_type=jnp.float32)
    band_slope = (band_prob * (band_back - row_dot[:, None])).astype(jnp.bfloat16)
    summary_slope = (summary_prob * (summary_back - row_dot[:, None])).astype(jnp.bfloat16)
    grad_query = (
        jnp.dot(band_slope, band_keys, preferred_element_type=jnp.float32)
        + jnp.dot(summary_slope, block_summary_keys, preferred_element_type=jnp.float32)
    ) * scale
    grad_key = jnp.dot(band_slope.T, query, preferred_element_type=jnp.float32) * scale
    grad_value = jnp.dot(band_low.T, grad_out, preferred_element_type=jnp.float32)
    grad_sum_key = jnp.dot(summary_slope.T, query, preferred_element_type=jnp.float32) * scale
    grad_sum_value = jnp.dot(summary_low.T, grad_out, preferred_element_type=jnp.float32)
    return (
        attended,
        grad_query,
        grad_key,
        grad_value,
        grad_sum_key,
        grad_sum_value,
        row_top,
        row_total,
        row_dot,
    )


def split_heads(block_rows, depth):
    return block_rows.reshape(block_rows.shape[0], -1, depth).transpose(1, 0, 2)


def merge_heads(head_rows, groups):
    number, row_count, depth = head_rows.shape
    return head_rows.transpose(1, 0, 2).reshape(row_count, groups, number // groups * depth)


def fold_heads(head_rows, groups):
    number, row_count, depth = head_rows.shape
    return (
        head_rows.reshape(groups, number // groups, row_count, depth).sum(axis=1).transpose(1, 0, 2)
    )


def repeat_heads(rows_first, head_count):
    return jnp.repeat(rows_first.transpose(1, 0, 2), head_count, axis=0)


def attend(query_x, key_x, value_x, grad_x):
    tokens, groups, depth = key_x.shape
    head_count = query_x.shape[2] // depth
    blocks = tokens // BLOCK_POSITIONS
    scaled = grad_x * 16
    edge_keys, edge_values = from_behind((key_x, value_x), "ctx", 1)
    pooled_keys = (
        jnp.sum(key_x.reshape(blocks, BLOCK_POSITIONS, groups, depth), axis=1, dtype=jnp.float32)
        / BLOCK_POSITIONS
    ).astype(jnp.bfloat16)
    pooled_values = (
        jnp.sum(value_x.reshape(blocks, BLOCK_POSITIONS, groups, depth), axis=1, dtype=jnp.float32)
        / BLOCK_POSITIONS
    ).astype(jnp.bfloat16)
    block_summary_keys, block_summary_values = (
        lax.all_gather(pooled_keys, "ctx", axis=0, tiled=True),
        lax.all_gather(pooled_values, "ctx", axis=0, tiled=True),
    )
    number = block_summary_keys.shape[0]
    summary_key_heads = repeat_heads(block_summary_keys, head_count)
    summary_value_heads = repeat_heads(block_summary_values, head_count)
    anchor = lax.axis_index("ctx") * tokens
    first_keep = 2 * BLOCK_POSITIONS
    key_grads = [jnp.zeros((BLOCK_POSITIONS, groups, depth), jnp.float32)]
    value_grads = [jnp.zeros((BLOCK_POSITIONS, groups, depth), jnp.float32)]
    block = 0
    lower = block * BLOCK_POSITIONS
    band_keys = jnp.concatenate([edge_keys, key_x], axis=0)
    band_values = jnp.concatenate([edge_values, value_x], axis=0)
    query_heads = split_heads(query_x, depth)
    grad_heads = split_heads(scaled, depth)
    first = anchor + lower
    term_list = lax.map(
        lambda items: head_terms(*items, first, first_keep),
        (
            query_heads,
            grad_heads,
            repeat_heads(band_keys, head_count),
            repeat_heads(band_values, head_count),
            summary_key_heads,
            summary_value_heads,
        ),
    )
    outputs = merge_heads(term_list[0], groups)
    query_grads = merge_heads(term_list[1], groups)
    local_key_gradient = fold_heads(term_list[2], groups)
    local_value_gradient = fold_heads(term_list[3], groups)
    key_grads[block] = local_key_gradient[first_keep - BLOCK_POSITIONS :]
    value_grads[block] = local_value_gradient[first_keep - BLOCK_POSITIONS :]
    edge_key_grad = local_key_gradient[:BLOCK_POSITIONS]
    edge_value_grad = local_value_gradient[:BLOCK_POSITIONS]
    summary_key_grad = term_list[4].reshape(groups, head_count, number, depth).sum(axis=1)
    summary_value_grad = term_list[5].reshape(groups, head_count, number, depth).sum(axis=1)
    later_keys, later_values = from_behind((edge_key_grad, edge_value_grad), "ctx", -1)
    key_grads[blocks - 1] = key_grads[blocks - 1] + later_keys
    value_grads[blocks - 1] = value_grads[blocks - 1] + later_values
    key_totals, value_totals = lax.psum((summary_key_grad, summary_value_grad), "ctx")
    start_offset = lax.axis_index("ctx") * blocks
    share_keys = lax.dynamic_slice_in_dim(key_totals, start_offset, blocks, 1)
    share_values = lax.dynamic_slice_in_dim(value_totals, start_offset, blocks, 1)
    block = 0
    key_grads[block] = key_grads[block] + share_keys[:, block, :][None] / BLOCK_POSITIONS
    value_grads[block] = value_grads[block] + share_values[:, block, :][None] / BLOCK_POSITIONS
    attended = outputs.astype(jnp.bfloat16)
    grad_queries = query_grads.astype(jnp.bfloat16)
    grad_keys = key_grads[0].astype(jnp.bfloat16)
    grad_values = value_grads[0].astype(jnp.bfloat16)
    return (attended, grad_queries, grad_keys, grad_values)


def finish(arrays):
    query_x, key_x, value_x, grad_x = arrays
    layer_outputs = attend(query_x[:, 0], key_x[:, 0], value_x[:, 0], grad_x[:, 0])
    return (
        lax.all_to_all(layer_outputs[0][:, None], "head", split_axis=0, concat_axis=1, tiled=True),
        lax.all_to_all(layer_outputs[1][:, None], "head", split_axis=0, concat_axis=1, tiled=True),
        lax.all_to_all(layer_outputs[2][:, None], "head", split_axis=0, concat_axis=1, tiled=True),
        lax.all_to_all(layer_outputs[3][:, None], "head", split_axis=0, concat_axis=1, tiled=True),
    )


def shards(queries, keys, values, cotangent):
    row_count = queries.shape[0]
    part_count = lax.axis_size("head")
    each_part_size = KEY_VALUE_HEADS // part_count
    head_count = QUERY_HEADS // KEY_VALUE_HEADS
    query_split = queries.reshape(row_count, part_count, each_part_size, head_count * HEAD_FEATURES)
    key_split = keys.reshape(row_count, part_count, each_part_size, HEAD_FEATURES)
    value_split = values.reshape(row_count, part_count, each_part_size, HEAD_FEATURES)
    grad_split = cotangent.reshape(
        row_count, part_count, each_part_size, head_count * HEAD_FEATURES
    )
    moved = (
        lax.all_to_all(query_split, "head", split_axis=1, concat_axis=0, tiled=True),
        lax.all_to_all(key_split, "head", split_axis=1, concat_axis=0, tiled=True),
        lax.all_to_all(value_split, "head", split_axis=1, concat_axis=0, tiled=True),
        lax.all_to_all(grad_split, "head", split_axis=1, concat_axis=0, tiled=True),
    )
    layer_outputs = finish(moved)
    return (
        layer_outputs[0].reshape(row_count, QUERY_HEADS * HEAD_FEATURES),
        layer_outputs[1].reshape(row_count, QUERY_HEADS * HEAD_FEATURES),
        layer_outputs[2].reshape(row_count, KEY_VALUE_HEADS * HEAD_FEATURES),
        layer_outputs[3].reshape(row_count, KEY_VALUE_HEADS * HEAD_FEATURES),
    )


def solution(mesh):
    placed = (
        P(("ctx", "head"), None),
        P(("ctx", "head"), None),
        P(("ctx", "head"), None),
        P(("ctx", "head"), None),
    )
    return jax.shard_map(
        shards,
        mesh=mesh,
        in_specs=placed,
        out_specs=(
            P(("ctx", "head"), None),
            P(("ctx", "head"), None),
            P(("ctx", "head"), None),
            P(("ctx", "head"), None),
        ),
        check_vma=False,
    )
```

profile of v0, /device:TPU:1, one launch (start us, length us, event | category | flops | bytes accessed | tf_op | source)
XLA Modules:
  0.0 1171.6 jit_solution(8070307337522854301)
XLA Ops:
  7.2 1.9 copy.93
  9.1 6.6 all-to-all-start.1
  15.7 1.8 copy.96
  17.5 4.9 all-to-all-done.1
  22.3 4.2 all-to-all-start.2
  29.2 4.1 all-to-all-done.2
  33.3 4.4 all-to-all-start
  39.0 13.7 %all-to-all-done = bf16[128,4,2,512]{3,2,0,1:T(2,128)(2,1)S(1)} async-done(((bf16[128,4,2,512]{3,2,0,1:T(2,128)(2,1)}), bf16[128,4,2,512]{3,2,0,1:T(2,128)(2,1)S(1)}, u32[]{:S(2)}, u32[]{:S(2)}) %all-to-all-start) | async-done | bytes 1048608 | tf_op jit(solution)/shard_map/all_to_all | solution.py:188
  52.7 4.4 all-to-all-start.3
  57.1 134.8 %all-gather.2 = bf16[64,2,128]{2,1,0:T(2,128)(2,1)S(1)} all-gather(bf16[1,2,128]{2,1,0:T(2,128)(2,1)S(1)} %fusion.73), channel_id=2, replica_groups=mesh['ctx'=64,'head'=4] {'ctx'}, dimensions={0}, use_global_device_ids=true | all-gather | bytes 33280 | tf_op jit(solution)/shard_map/all_gather | solution.py:110
  195.6 121.2 %all-gather.3 = bf16[64,2,128]{2,1,0:T(2,128)(2,1)S(1)} all-gather(bf16[1,2,128]{2,1,0:T(2,128)(2,1)S(1)} %fusion.74), channel_id=3, replica_groups=mesh['ctx'=64,'head'=4] {'ctx'}, dimensions={0}, use_global_device_ids=true | all-gather | bytes 33280 | tf_op jit(solution)/shard_map/all_gather | solution.py:111
  328.3 167.9 %while.23 = (s32[]{:T(128)}, bf16[8,512,128]{1,2,0:T(8,128)(2,1)}, bf16[8,512,128]{1,2,0:T(8,128)(2,1)}, f32[8,1024,128]{2,1,0:T(8,128)}, f32[8,1024,128]{2,1,0:...) while((s32[]{:T(128)}, bf16[8,512,128]{1,2,0:T(8,128)(2,1)}, ...), condition=%wide.region_8.9_spmd, body=%wide.region_2.8_spmd.sunk | while | flops 868427840 | bytes 26759680 | solution.py:127
  329.4 1.8 select_reduce_fusion.4
  344.9 2.2 fusion.134
  347.1 2.2 fusion.133
  350.4 1.8 select_reduce_fusion.4
  365.9 2.2 fusion.134
  368.1 2.2 fusion.133
  371.4 1.8 select_reduce_fusion.4
  386.9 2.2 fusion.134
  389.1 2.2 fusion.133
  392.4 1.8 select_reduce_fusion.4
  407.9 2.2 fusion.134
  410.1 2.2 fusion.133
  413.4 1.8 select_reduce_fusion.4
  428.9 2.2 fusion.134
  431.1 2.2 fusion.133
  434.4 1.8 select_reduce_fusion.4
  449.8 2.2 fusion.134
  452.1 2.2 fusion.133
  455.4 1.8 select_reduce_fusion.4
  470.8 2.2 fusion.134
  473.0 2.2 fusion.133
  476.3 1.8 select_reduce_fusion.4
  491.8 2.2 fusion.134
  494.0 2.2 fusion.133
  496.2 4.2 bitcast_reduce_fusion
  505.7 561.4 %all-reduce.3.cloned.1.call-done = (f32[2,64,128]{2,1,0:T(8,128)}, f32[2,64,128]{2,1,0:T(8,128)}) async-done(((f32[2,64,128]{2,1,0:T(8,128)}, f32[2,64,128]{2,1,0:T(8,128)}), (f32[2,64,128]{2,1,0:T(8,128)}, f32[2,64,128]{2,1,0:T(8,128)})) %all-reduce.3.cloned.1.call-update) | async-done | bytes 131088 | tf_op jit(solution)/shard_map/psum | solution.py:151
  1069.6 36.4 %all-to-all-start.7 = ((bf16[512,1,2,128]{3,2,1,0:T(2,128)(2,1)}), bf16[512,1,2,128]{3,2,1,0:T(2,128)(2,1)S(1)}, u32[]{:S(2)}, u32[]{:S(2)}) async-start(bf16[512,1,2,128]{3,2,1,0:T(2,128)(2,1)} %copy.114), calls=%async_computation.7 | async-start | bytes 524288 | tf_op jit(solution)/shard_map/all_to_all | solution.py:172
  1108.1 4.6 all-to-all-done.7
  1112.7 4.2 all-to-all-start.6
  1117.0 3.7 copy.104
  1120.7 2.9 all-to-all-done.6
  1123.7 4.4 all-to-all-start.4
  1128.0 2.1 copy.108
  1130.1 13.0 %all-to-all-done.4 = bf16[512,1,2,512]{3,2,1,0:T(2,128)(2,1)S(1)} async-done(((bf16[512,1,2,512]{3,2,1,0:T(2,128)(2,1)}), bf16[512,1,2,512]{3,2,1,0:T(2,128)(2,1)S(1)}, u32[]{:S(2)}, u32[]{:S(2)}) %all-to-all-start.4) | async-done | bytes 1048608 | tf_op jit(solution)/shard_map/all_to_all | solution.py:169
  1143.1 4.4 all-to-all-start.5
  1151.8 10.8 all-to-all-done.5
  (275 shorter events, 153.0 us)
Async XLA Ops:
  7.2 19.4 %copy-start.2 = (bf16[128,4096]{1,0:T(8,128)(2,1)S(1)}, bf16[128,4096]{1,0:T(8,128)(2,1)}, u32[]{:S(2)}) copy-start(bf16[128,4096]{1,0:T(8,128)(2,1)} %param.6) | copy-start | bytes 3145732
  9.1 13.3 %all-to-all-start.1 = ((bf16[128,4,2,128]{0,3,2,1:T(8,128)(2,1)}), bf16[128,4,2,128]{0,3,2,1:T(8,128)(2,1)S(1)}, u32[]{:S(2)}, u32[]{:S(2)}) async-start(bf16[128,4,2,128]{0,3,2,1:T(8,128)(2,1)} %bitcast.15), calls=%async_computation.1 | async-start | bytes 524288 | tf_op jit(solution)/shard_map/all_to_all | solution.py:189
  22.3 10.9 all-to-all-start.2
  27.4 10.2 copy-start.3
  33.3 19.5 %all-to-all-start = ((bf16[128,4,2,512]{3,2,0,1:T(2,128)(2,1)}), bf16[128,4,2,512]{3,2,0,1:T(2,128)(2,1)S(1)}, u32[]{:S(2)}, u32[]{:S(2)}) async-start(bf16[128,4,2,512]{3,2,0,1:T(2,128)(2,1)} %copy.92), calls=%async_computation | async-start | bytes 2097152 | tf_op jit(solution)/shard_map/all_to_all | solution.py:188
  52.7 268.4 %all-to-all-start.3 = ((bf16[128,4,2,512]{0,3,2,1:T(8,128)(2,1)}), bf16[128,4,2,512]{0,3,2,1:T(8,128)(2,1)S(1)}, u32[]{:S(2)}, u32[]{:S(2)}) async-start(bf16[128,4,2,512]{0,3,2,1:T(8,128)(2,1)} %bitcast.35), calls=%async_computation.3 | async-start | bytes 2097152 | tf_op jit(solution)/shard_map/all_to_all | solution.py:191
  57.1 1010.1 %all-reduce.3.cloned.1.call-start = ((), (), s32[]{:S(2)}) async-start(), calls=%async_computation.8 | async-start | bytes 262144 | tf_op jit(solution)/shard_map/psum | solution.py:151
  192.9 124.6 %collective-permute-start.1 = (bf16[512,2,128]{2,0,1:T(8,128)(2,1)S(1)}, bf16[512,2,128]{2,0,1:T(8,128)(2,1)S(1)}, u32[]{:S(2)}, u32[]{:S(2)}) collective-permute-start(bf16[512,2,128]{2,0,1:T(8,128)(2,1)S(1)} %bitcast.226), channel_id=1, source_target_pairs={{0,4},{4,8},{8,12},{12,16},{16,20},{20,24},{24,28},{28,32},{32,36}... | collective-permute-start | bytes 786440 | tf_op jit(solution)/shard_map/ppermute | solution.py:18
  194.2 124.1 %collective-permute-start = (bf16[512,2,128]{2,0,1:T(8,128)(2,1)S(1)}, bf16[512,2,128]{2,0,1:T(8,128)(2,1)S(1)}, u32[]{:S(2)}, u32[]{:S(2)}) collective-permute-start(bf16[512,2,128]{2,0,1:T(8,128)(2,1)S(1)} %bitcast.224), channel_id=1, source_target_pairs={{0,4},{4,8},{8,12},{12,16},{16,20},{20,24},{24,28},{28,32},{32,36}... | collective-permute-start | bytes 786440 | tf_op jit(solution)/shard_map/ppermute | solution.py:18
  322.1 2.3 copy-start.7
  322.1 2.3 copy-start.8
  322.1 3.0 copy-start.1
  322.8 3.9 copy-start
  335.6 6.9 copy-start.5
  344.9 4.4 copy-start.6
  356.6 6.9 copy-start.5
  365.9 4.4 copy-start.6
  377.6 6.9 copy-start.5
  386.9 4.4 copy-start.6
  398.6 6.9 copy-start.5
  407.9 4.4 copy-start.6
  419.6 6.9 copy-start.5
  428.9 4.4 copy-start.6
  440.5 6.9 copy-start.5
  449.8 4.4 copy-start.6
  461.5 6.9 copy-start.5
  470.8 4.4 copy-start.6
  482.5 6.9 copy-start.5
  491.8 4.4 copy-start.6
  500.5 568.1 %collective-permute-start.3 = (f32[512,2,128]{2,0,1:T(8,128)S(1)}, f32[512,2,128]{2,0,1:T(8,128)S(1)}, u32[]{:S(2)}, u32[]{:S(2)}) collective-permute-start(f32[512,2,128]{2,0,1:T(8,128)S(1)} %slice.19), channel_id=1, source_target_pairs={{4,0},{8,4},{12,8},{16,12},{20,16},{24,20},{28,24},{32,28},{36,32}... | collective-permute-start | bytes 1572872 | tf_op jit(solution)/shard_map/ppermute | solution.py:18
  504.3 601.8 %collective-permute-start.2 = (f32[512,2,128]{2,0,1:T(8,128)}, f32[512,2,128]{2,0,1:T(8,128)}, u32[]{:S(2)}, u32[]{:S(2)}) collective-permute-start(f32[512,2,128]{2,0,1:T(8,128)} %slice.17), channel_id=1, source_target_pairs={{4,0},{8,4},{12,8},{16,12},{20,16},{24,20},{28,24},{32,28},{36,32}... | collective-permute-start | bytes 1572872 | tf_op jit(solution)/shard_map/ppermute | solution.py:18
  1069.6 43.1 %all-to-all-start.7 = ((bf16[512,1,2,128]{3,2,1,0:T(2,128)(2,1)}), bf16[512,1,2,128]{3,2,1,0:T(2,128)(2,1)S(1)}, u32[]{:S(2)}, u32[]{:S(2)}) async-start(bf16[512,1,2,128]{3,2,1,0:T(2,128)(2,1)} %copy.114), calls=%async_computation.7 | async-start | bytes 524288 | tf_op jit(solution)/shard_map/all_to_all | solution.py:172
  1112.7 10.9 all-to-all-start.6
  1117.0 11.0 copy-start.4
  1123.7 19.5 %all-to-all-start.4 = ((bf16[512,1,2,512]{3,2,1,0:T(2,128)(2,1)}), bf16[512,1,2,512]{3,2,1,0:T(2,128)(2,1)S(1)}, u32[]{:S(2)}, u32[]{:S(2)}) async-start(bf16[512,1,2,512]{3,2,1,0:T(2,128)(2,1)} %copy.104), calls=%async_computation.4 | async-start | bytes 2097152 | tf_op jit(solution)/shard_map/all_to_all | solution.py:169
  1143.1 19.5 %all-to-all-start.5 = ((bf16[512,1,2,512]{3,2,1,0:T(2,128)(2,1)}), bf16[512,1,2,512]{3,2,1,0:T(2,128)(2,1)S(1)}, u32[]{:S(2)}, u32[]{:S(2)}) async-start(bf16[512,1,2,512]{3,2,1,0:T(2,128)(2,1)} %copy.108), calls=%async_computation.5 | async-start | bytes 2097152 | tf_op jit(solution)/shard_map/all_to_all | solution.py:170
Sparse Core Ops, SparseCore 0:
  503.5 563.5 all-reduce.2
where the time goes:
time: 1180 us; the launch traced here: 1170 us
  waiting for transfers between devices  615 us (52%)
  blocking collectives  256 us (22%)
  matrix products  139 us (12%)
  starting transfers between devices  74.3 us (6%)
  local copies, waits for them, and re-layouts  39.4 us (3%)
  other arithmetic  32.8 us (3%)
  between operations  14.3 us (1%)
    psum x1, waiting for transfers between devices, attend(): lax.psum((summary_key_grad, summary_value_grad), 'ctx')  561 us
    all_gather x1, blocking collectives, attend(): lax.all_gather(pooled_keys, 'ctx', axis=0, tiled=True)  135 us
    all_gather x1, blocking collectives, attend(): lax.all_gather(pooled_values, 'ctx', axis=0, tiled=True)  121 us
    all_to_all x1, starting transfers between devices, finish(): lax.all_to_all(layer_outputs[3][:, None], 'head', split_axis=0, concat_ax...  36.4 us
  transfers between devices with their start and end apart: 13, of which 8 were waited for; matrix products, arithmetic and copies ran while one was open for 2% of the time, Pallas kernels for 0%

commit v1 on v0

v1 whole, which is shorter than its diff:
```python
import math

import jax
import jax.numpy as jnp
from jax import lax
from jax.experimental import pallas as pl
from jax.experimental.pallas import tpu as pltpu
from jax.sharding import PartitionSpec as P

MESH = pl.DeviceIdType.MESH
F32 = jnp.float32
BF16 = jnp.bfloat16

D = 128
BLOCK = 512
ROWS = 128
CHIP = 256
GROUPS = 4
REPEAT = 4
KCOLS = GROUPS * D
QCOLS = GROUPS * REPEAT * D
BAND = 4 * CHIP
NX, NY, NZ = 4, 4, 8
NCTX = 64
LOWEST = -1e30
SCALE = 1.0 / math.sqrt(D)
LOG2 = SCALE / math.log(2.0)


def dot(a, b):
    return jnp.dot(a, b, preferred_element_type=F32)


def dot_t(a, b):
    return lax.dot_general(a, b, (((1,), (1,)), ((), ())), preferred_element_type=F32)


def al(index, size):
    return pl.multiple_of(index * size, size)


def kernel(
    q_in, k_in, v_in, do_in, out_ref, gq_ref, gk_ref, gv_ref,
    qb, dob, kv, kvt, probs, ob, gqb, db, stats, outb, gqout,
    xs, sumb, sg, rsz, rsy, rsx, acc1, acc2, acc3,
    dkv, own, gsend, grecv, fin,
    kv_send, kv_recv, q_send, do_send, q_recv, do_recv,
    xs_send, xs_recv, ys_send, ys_recv, zs_send, zs_recv,
    rz_send, rz_recv, ry_send, ry_recv, rx_send, rx_recv,
    g_send, g_recv, o_send, o_recv, o_local, f_send, f_recv, f_local,
):
    ctx = lax.axis_index("ctx")
    head = lax.axis_index("head")
    core = lax.rem(head, 2)
    xh = lax.div(head, 2)
    xl = lax.rem(ctx, 2)
    y = lax.rem(lax.div(ctx, 2), NY)
    z = lax.div(ctx, 2 * NY)
    x = xh * 2 + xl
    sister = (ctx, xh * 2 + 1 - core)
    after = lax.rem(ctx + 1, NCTX)
    before = lax.rem(ctx + NCTX - 1, NCTX)

    def at_x(d):
        other = lax.rem(x + d, NX)
        return other, (z * (2 * NY) + y * 2 + lax.rem(other, 2), lax.div(other, 2) * 2 + core)

    def at_y(d):
        other = lax.rem(y + d, NY)
        return other, (z * (2 * NY) + other * 2 + xl, head)

    def at_z(d):
        other = lax.rem(z + d, NZ)
        return other, (other * (2 * NY) + y * 2 + xl, head)

    def send(src, dst, send_sem, recv_sem, device):
        pltpu.make_async_remote_copy(
            src_ref=src, dst_ref=dst, send_sem=send_sem, recv_sem=recv_sem, device_id=device, device_id_type=MESH
        ).start()

    def local(src, dst, sem):
        pltpu.make_async_copy(src, dst, sem).start()

    def wait(ref, sem):
        pltpu.make_async_copy(ref, ref, sem).wait()

    my_rows = pl.ds(al(core, ROWS), ROWS)
    her_rows = pl.ds(al(1 - core, ROWS), ROWS)

    for g in range(GROUPS):
        for i, ref in enumerate((k_in, v_in)):
            local(
                ref.at[:, pl.ds(al(core * GROUPS + g, D), D)],
                kv.at[i, pl.ds(al(6 + core, ROWS), ROWS), pl.ds(g * D, D)],
                kv_recv.at[3, g],
            )
    for g in range(GROUPS):
        for ref, buf, sem in ((q_in, qb, q_recv), (do_in, dob, do_recv)):
            local(
                ref.at[:, pl.ds(al(core * GROUPS + g, REPEAT * D), REPEAT * D)],
                buf.at[my_rows, pl.ds(g * REPEAT * D, REPEAT * D)],
                sem.at[g],
            )

    @pl.when(xh == 0)
    def _():
        kv[:, 2 * CHIP : 3 * CHIP, :] = jnp.zeros((2, CHIP, KCOLS), BF16)

    barrier = pltpu.get_barrier_semaphore()
    partners = [sister]
    partners += [(ctx, (1 - xh) * 2 + c) for c in range(2)]
    partners += [(c, h) for c in (after, before) for h in range(4)]
    partners += [at_y(d)[1] for d in range(1, NY)] + [at_z(d)[1] for d in range(1, NZ)]
    for device in partners:
        pl.semaphore_signal(barrier, inc=1, device_id=device, device_id_type=MESH)
    pl.semaphore_wait(barrier, len(partners))

    def send_kv(g, slot, half, sem, device):
        for i, ref in enumerate((k_in, v_in)):
            send(
                ref.at[:, pl.ds(al(half * GROUPS + g, D), D)],
                kv.at[i, pl.ds(al(slot * 2 + core, ROWS), ROWS), pl.ds(g * D, D)],
                kv_send.at[sem],
                kv_recv.at[slot, g],
                device,
            )

    for g in range(GROUPS):
        send_kv(g, 3, 1 - core, 0, sister)

    for g in range(GROUPS):

        @pl.when(xh == 0)
        def _():
            for c in range(2):
                send_kv(g, 2, c, 1 + c, (ctx, 2 + c))

        for h in range(4):
            send_kv(g, xh, h % 2, 3 + h, (after, h))
        send(
            q_in.at[:, pl.ds(al((1 - core) * GROUPS + g, REPEAT * D), REPEAT * D)],
            qb.at[my_rows, pl.ds(g * REPEAT * D, REPEAT * D)],
            q_send.at[g], q_recv.at[g], sister,
        )
    for g in range(GROUPS):
        send(
            do_in.at[:, pl.ds(al((1 - core) * GROUPS + g, REPEAT * D), REPEAT * D)],
            dob.at[my_rows, pl.ds(g * REPEAT * D, REPEAT * D)],
            do_send.at[g], do_recv.at[g], sister,
        )

    for g in range(GROUPS):
        wait(kv.at[:, pl.ds(3 * CHIP, CHIP), pl.ds(g * D, D)], kv_recv.at[3, g])
    pieces = []
    for i in range(2):
        total = jnp.sum(kv[i, 3 * CHIP :, :].astype(F32), axis=0, keepdims=True)
        pieces += [total[:, g * D : (g + 1) * D] for g in range(GROUPS)]
    xs[0] = jnp.concatenate(pieces, axis=0)
    for d in range(1, NX):
        send(xs.at[0], xs.at[d], xs_send.at[d], xs_recv.at[d], at_x(d)[1])

    def summaries_along_y():
        for d in range(1, NX):
            wait(xs.at[d], xs_recv.at[d])
        mine = (xs[0] + xs[2]) / BLOCK
        others = (xs[1] + xs[3]) / BLOCK
        first = z * (2 * NY) + y * 2
        sumb[pl.ds(al(first + xl, 8), 8), :] = mine.astype(BF16).astype(F32)
        sumb[pl.ds(al(first + 1 - xl, 8), 8), :] = others.astype(BF16).astype(F32)
        rows = pl.ds(al(z * NY + y, 16), 16)
        for d in range(1, NY):
            send(sumb.at[rows, :], sumb.at[rows, :], ys_send.at[d], ys_recv.at[d], at_y(d)[1])

    def summaries_along_z():
        for d in range(1, NY):
            wait(sumb.at[pl.ds(0, 16), :], ys_recv.at[d])
        rows = pl.ds(al(z, 64), 64)
        for d in range(1, NZ):
            send(sumb.at[rows, :], sumb.at[rows, :], zs_send.at[d], zs_recv.at[d], at_z(d)[1])

    def summaries_arrived():
        for d in range(1, NZ):
            wait(sumb.at[pl.ds(0, 64), :], zs_recv.at[d])

    no_before = jnp.where(ctx == 0, LOWEST, 0.0).astype(F32)
    no_partner = jnp.where(xh == 0, LOWEST, 0.0).astype(F32)
    causal = lax.broadcasted_iota(jnp.int32, (CHIP, CHIP), 0) <= lax.broadcasted_iota(jnp.int32, (CHIP, CHIP), 1)

    def band_forward(g):
        group = pl.ds(g * D, D)
        for slot in range(2):
            wait(kv.at[:, pl.ds(slot * CHIP, CHIP), group], kv_recv.at[slot, g])

        @pl.when(xh == 1)
        def _():
            wait(kv.at[:, pl.ds(2 * CHIP, CHIP), group], kv_recv.at[2, g])

        wait(qb.at[:, pl.ds(g * REPEAT * D, REPEAT * D)], q_recv.at[g])
        for i in range(2):
            kvt[i, g] = kv[i, :, g * D : (g + 1) * D].T

        def one(j, carry):
            h = g * REPEAT + j
            q = qb[:, pl.ds(al(h, D), D)]
            s = dot_t(kv[0, :, g * D : (g + 1) * D], q)
            s_before, s_partner = s[: 2 * CHIP], s[2 * CHIP : 3 * CHIP]
            s_own = jnp.where(causal, s[3 * CHIP :], LOWEST)
            top = jnp.maximum(
                jnp.maximum(
                    jnp.max(s_before, axis=0, keepdims=True) + no_before,
                    jnp.max(s_partner, axis=0, keepdims=True) + no_partner,
                ),
                jnp.max(s_own, axis=0, keepdims=True),
            ) * LOG2
            w_before = jnp.exp2(s_before * LOG2 - (top - no_before))
            w_partner = jnp.exp2(s_partner * LOG2 - (top - no_partner))
            w_own = jnp.exp2(s_own * LOG2 - top)
            total = (
                jnp.sum(w_before, axis=0, keepdims=True)
                + jnp.sum(w_partner, axis=0, keepdims=True)
                + jnp.sum(w_own, axis=0, keepdims=True)
            )
            probs[h, : 2 * CHIP, :] = w_before.astype(BF16)
            probs[h, 2 * CHIP : 3 * CHIP, :] = w_partner.astype(BF16)
            probs[h, 3 * CHIP :, :] = w_own.astype(BF16)
            ob[h] = dot(kvt[1, g], probs[h])
            stats[h, 0:1, :] = top
            stats[h, 1:2, :] = total
            return carry

        lax.fori_loop(0, REPEAT, one, 0)

    seen = lax.broadcasted_iota(jnp.int32, (NCTX, CHIP), 0) < ctx

    def summary_part(g):
        sum_k = sumb[pl.ds(g, NCTX, stride=8), :]
        sum_v = sumb[pl.ds(GROUPS + g, NCTX, stride=8), :]
        sum_kt, sum_vt = sum_k.T.astype(BF16), sum_v.T.astype(BF16)
        sum_k, sum_v = sum_k.astype(BF16), sum_v.astype(BF16)
        wait(dob.at[:, pl.ds(g * REPEAT * D, REPEAT * D)], do_recv.at[g])

        def one(j, carry):
            grad_k, grad_v = carry
            h = g * REPEAT + j
            cols = pl.ds(al(h, D), D)
            q = qb[:, cols]
            s = jnp.where(seen, dot_t(sum_k, q), LOWEST)
            s_top = jnp.max(s, axis=0, keepdims=True) * LOG2
            w = jnp.where(seen, jnp.exp2(s * LOG2 - s_top), 0.0)
            b_top, b_total = stats[h, 0:1, :], stats[h, 1:2, :]
            top = jnp.maximum(s_top, b_top)
            b_part, s_part = jnp.exp2(b_top - top), jnp.exp2(s_top - top)
            inverse = 1.0 / (b_part * b_total + s_part * jnp.sum(w, axis=0, keepdims=True))
            b_part, s_part = b_part * inverse, s_part * inverse
            w_low = w.astype(BF16)
            attended = ob[h] * b_part + dot(sum_vt, w_low) * s_part
            outb[:, cols] = attended.T.astype(BF16)
            grad_out = dob[:, cols].astype(F32).T
            b_grad = (grad_out * (16.0 * b_part)).astype(BF16)
            s_grad = (grad_out * (16.0 * s_part)).astype(BF16)
            db[h] = b_grad
            stats[h, 2:3, :] = jnp.sum(b_grad.astype(F32) * attended, axis=0, keepdims=True)
            s_dot = jnp.sum(s_grad.astype(F32) * attended, axis=0, keepdims=True)
            slope = (w * (dot(sum_v, s_grad) - s_dot)).astype(BF16)
            gqb[h] = dot(sum_kt, slope)
            return grad_k + dot(slope, q), grad_v + dot_t(w_low, s_grad)

        zero = jnp.zeros((NCTX, D), F32)
        grad_k, grad_v = lax.fori_loop(0, REPEAT, one, (zero, zero))
        sg[pl.ds(g, NCTX, stride=8), :] = grad_k * SCALE
        sg[pl.ds(GROUPS + g, NCTX, stride=8), :] = grad_v

    def give(buf, ref, g, which):
        cols = pl.ds(g * REPEAT * D, REPEAT * D)
        out_cols = pl.ds(al(core * GROUPS + g, REPEAT * D), REPEAT * D)
        send(buf.at[her_rows, cols], ref.at[:, out_cols], o_send.at[which, g], o_recv.at[which, g], sister)
        local(buf.at[my_rows, cols], ref.at[:, out_cols], o_local.at[which, g])

    def grads_along_z():
        for d in range(1, NZ):
            other, device = at_z(d)
            send(sg.at[pl.ds(al(other, 64), 64), :], rsz.at[d], rz_send.at[d], rz_recv.at[d], device)

    def grads_along_y():
        for d in range(1, NZ):
            wait(rsz.at[d], rz_recv.at[d])
        total = sg[pl.ds(al(z, 64), 64), :]
        for d in range(1, NZ):
            total = total + rsz[d]
        acc1[...] = total
        for d in range(1, NY):
            other, device = at_y(d)
            send(acc1.at[pl.ds(al(other, 16), 16), :], rsy.at[d], ry_send.at[d], ry_recv.at[d], device)

    def grads_along_x():
        for d in range(1, NY):
            wait(rsy.at[d], ry_recv.at[d])
        total = acc1[pl.ds(al(y, 16), 16), :]
        for d in range(1, NY):
            total = total + rsy[d]
        acc2[...] = total
        for d in range(1, NX):
            other, device = at_x(d)
            send(acc2.at[pl.ds(al(lax.rem(other, 2), 8), 8), :], rsx.at[d], rx_send.at[d], rx_recv.at[d], device)

    def grads_arrived():
        for d in range(1, NX):
            wait(rsx.at[d], rx_recv.at[d])
        total = acc2[pl.ds(al(xl, 8), 8), :]
        for d in range(1, NX):
            total = total + rsx[d]
        acc3[...] = total / BLOCK

    def band_backward(g):
        def one(j, carry):
            h = g * REPEAT + j
            cols = pl.ds(al(h, D), D)
            q = qb[:, cols]
            grad = db[h]
            back = dot(kv[1, :, g * D : (g + 1) * D], grad)
            low = probs[h]
            slope = (low.astype(F32) * (back - stats[h, 2:3, :])).astype(BF16)
            grad_q = (gqb[h] + dot(kvt[0, g], slope)) * SCALE
            gqout[:, cols] = grad_q.T.astype(BF16)
            grad_k = dot(slope, q)
            grad_v = dot_t(low, grad)

            @pl.when(j == 0)
            def _():
                dkv[0] = grad_k
                dkv[1] = grad_v

            @pl.when(j > 0)
            def _():
                dkv[0] += grad_k
                dkv[1] += grad_v

            return carry

        lax.fori_loop(0, REPEAT, one, 0)
        own[0, g] = dkv[0, 3 * CHIP :, :] * SCALE
        own[1, g] = dkv[1, 3 * CHIP :, :]
        for slot in range(3):
            gsend[slot, g, 0] = (dkv[0, slot * CHIP : (slot + 1) * CHIP, :] * SCALE).astype(BF16)
            gsend[slot, g, 1] = dkv[1, slot * CHIP : (slot + 1) * CHIP, :].astype(BF16)
        for slot in range(2):
            send(
                gsend.at[slot, g], grecv.at[xh, g], g_send.at[slot, g], g_recv.at[xh, g], (before, slot * 2 + core)
            )

        @pl.when(xh == 1)
        def _():
            send(gsend.at[2, g], grecv.at[2, g], g_send.at[2, g], g_recv.at[2, g], (ctx, core))

    def finish(g):
        for slot in range(2):
            wait(grecv.at[slot, g], g_recv.at[slot, g])

        @pl.when(xh == 0)
        def _():
            wait(grecv.at[2, g], g_recv.at[2, g])
            for i in range(2):
                own[i, g] += grecv[2, g, i].astype(F32)

        for i, ref in enumerate((gk_ref, gv_ref)):
            total = own[i, g] + grecv[0, g, i].astype(F32) + grecv[1, g, i].astype(F32)
            row = i * GROUPS + g
            fin[g, i] = (total + acc3[row : row + 1, :]).astype(BF16)
            cols = pl.ds(al(core * GROUPS + g, D), D)
            send(fin.at[g, i, her_rows, :], ref.at[:, cols], f_send.at[i, g], f_recv.at[i, g], sister)
            local(fin.at[g, i, my_rows, :], ref.at[:, cols], f_local.at[i, g])

    band_forward(0)
    summaries_along_y()
    band_forward(1)
    summaries_along_z()
    band_forward(2)
    band_forward(3)
    summaries_arrived()
    for g in range(GROUPS):
        summary_part(g)
        give(outb, out_ref, g, 0)
    grads_along_z()
    band_backward(0)
    give(gqout, gq_ref, 0, 1)
    grads_along_y()
    band_backward(1)
    give(gqout, gq_ref, 1, 1)
    grads_along_x()
    band_backward(2)
    give(gqout, gq_ref, 2, 1)
    grads_arrived()
    band_backward(3)
    give(gqout, gq_ref, 3, 1)
    for g in range(GROUPS):
        finish(g)

    rows_all = kv.at[:, pl.ds(0, ROWS), :]
    wait(rows_all, kv_send.at[0])
    for h in range(4):
        wait(rows_all, kv_send.at[3 + h])

    @pl.when(xh == 0)
    def _():
        for c in range(2):
            wait(rows_all, kv_send.at[1 + c])

    @pl.when(xh == 1)
    def _():
        for g in range(GROUPS):
            wait(gsend.at[2, g], g_send.at[2, g])

    part = qb.at[my_rows, pl.ds(0, REPEAT * D)]
    for g in range(GROUPS):
        wait(part, q_send.at[g])
        wait(part, do_send.at[g])
        for slot in range(2):
            wait(gsend.at[slot, g], g_send.at[slot, g])
        for i in range(2):
            wait(part, o_send.at[i, g])
            wait(part, o_recv.at[i, g])
            wait(part, o_local.at[i, g])
            wait(fin.at[g, i, my_rows, :], f_send.at[i, g])
            wait(fin.at[g, i, my_rows, :], f_recv.at[i, g])
            wait(fin.at[g, i, my_rows, :], f_local.at[i, g])
    for d in range(1, NX):
        wait(xs.at[d], xs_send.at[d])
        wait(rsx.at[d], rx_send.at[d])
    for d in range(1, NY):
        wait(rsy.at[d], ys_send.at[d])
        wait(rsy.at[d], ry_send.at[d])
    for d in range(1, NZ):
        wait(rsz.at[d], zs_send.at[d])
        wait(rsz.at[d], rz_send.at[d])


def shards(queries, keys, values, cotangent):
    heads = GROUPS * REPEAT
    dma = pltpu.SemaphoreType.DMA
    scratch = [
        pltpu.VMEM((CHIP, QCOLS), BF16),
        pltpu.VMEM((CHIP, QCOLS), BF16),
        pltpu.VMEM((2, BAND, KCOLS), BF16),
        pltpu.VMEM((2, GROUPS, D, BAND), BF16),
        pltpu.VMEM((heads, BAND, CHIP), BF16),
        pltpu.VMEM((heads, D, CHIP), F32),
        pltpu.VMEM((heads, D, CHIP), F32),
        pltpu.VMEM((heads, D, CHIP), BF16),
        pltpu.VMEM((heads, 8, CHIP), F32),
        pltpu.VMEM((CHIP, QCOLS), BF16),
        pltpu.VMEM((CHIP, QCOLS), BF16),
        pltpu.VMEM((NX, 8, D), F32),
        pltpu.VMEM((NCTX * 8, D), F32),
        pltpu.VMEM((NCTX * 8, D), F32),
        pltpu.VMEM((NZ, 64, D), F32),
        pltpu.VMEM((NY, 16, D), F32),
        pltpu.VMEM((NX, 8, D), F32),
        pltpu.VMEM((64, D), F32),
        pltpu.VMEM((16, D), F32),
        pltpu.VMEM((8, D), F32),
        pltpu.VMEM((2, BAND, D), F32),
        pltpu.VMEM((2, GROUPS, CHIP, D), F32),
        pltpu.VMEM((3, GROUPS, 2, CHIP, D), BF16),
        pltpu.VMEM((3, GROUPS, 2, CHIP, D), BF16),
        pltpu.VMEM((GROUPS, 2, CHIP, D), BF16),
        dma((7,)), dma((4, GROUPS)),
        dma((GROUPS,)), dma((GROUPS,)), dma((GROUPS,)), dma((GROUPS,)),
        dma((NX,)), dma((NX,)), dma((NY,)), dma((NY,)), dma((NZ,)), dma((NZ,)),
        dma((NZ,)), dma((NZ,)), dma((NY,)), dma((NY,)), dma((NX,)), dma((NX,)),
        dma((3, GROUPS)), dma((3, GROUPS)),
        dma((2, GROUPS)), dma((2, GROUPS)), dma((2, GROUPS)),
        dma((2, GROUPS)), dma((2, GROUPS)), dma((2, GROUPS)),
    ]
    anywhere = pl.BlockSpec(memory_space=pl.ANY)
    return pl.pallas_call(
        kernel,
        out_shape=[jax.ShapeDtypeStruct(a.shape, BF16) for a in (queries, cotangent, keys, values)],
        in_specs=[anywhere] * 4,
        out_specs=[anywhere] * 4,
        scratch_shapes=scratch,
        compiler_params=pltpu.CompilerParams(
            collective_id=0, has_side_effects=True, vmem_limit_bytes=56 * 1024 * 1024
        ),
    )(queries, keys, values, cotangent)


def solution(mesh):
    placed = P(("ctx", "head"), None)
    return jax.shard_map(
        shards, mesh=mesh, in_specs=(placed,) * 4, out_specs=(placed,) * 4, check_vma=False
    )
```

time: 1180 us -> 107 us (0.09)
  waiting for transfers between devices: 615 us -> 0 us
  blocking collectives: 256 us -> 0 us
  matrix products: 139 us -> 0 us
  Pallas kernels: 0 us -> 99.7 us
  starting transfers between devices: 74.3 us -> 0 us
  local copies, waits for them, and re-layouts: 39.4 us -> 5.22 us
  other arithmetic: 32.8 us -> 0 us
  between operations: 14.3 us -> 0.65 us
    psum x1 -> x0, waiting for transfers between devices: 561 us -> none  [attend(): lax.psum((summary_key_grad, summary_value_grad), 'ctx')]
    all_gather x2 -> x0, blocking collectives: 256 us -> none  [the longest x1 135 us: attend(): lax.all_gather(pooled_keys, 'ctx', axis=0, tiled=True)]
    dot_general x96 -> x0, matrix products: 139 us -> none  [the longest x8 17.8 us: head_terms(): jnp.dot(band_low.T, grad_out, preferred_element_type=jnp.float32)]
    pallas_call x0 -> x1, Pallas kernels: none -> 99.7 us  [shards(): pl.pallas_call(kernel, out_shape=[jax.ShapeDtypeStruct(a.shape, BF16) for...]
    all_to_all x8 -> x0, starting transfers between devices: 69 us -> none  [the longest x1 36.4 us: finish(): lax.all_to_all(layer_outputs[3][:, None], 'head', split_axis=0, concat_ax...]
    all_to_all x8 -> x0, waiting for transfers between devices: 54 us -> none  [the longest x1 13.7 us: shards(): lax.all_to_all(query_split, 'head', split_axis=1, concat_axis=0, tiled=True)]
    reduce_sum x28 -> x0, other arithmetic: 21.5 us -> none  [the longest x16 7.72 us: head_terms(): row_total = jnp.sum(band_weight, axis=1) + jnp.sum(summary_weight, axis=1)]
  transfers between devices with their start and end apart: 13 -> 0, of which waited for: 8 -> 0; matrix products, arithmetic and copies ran while one was open for 2% -> 0% of each run, Pallas kernels for 0% -> 0%
where the time goes in v1:
time: 107 us; the launch traced here: 106 us
  Pallas kernels  99.7 us (93%)
  local copies, waits for them, and re-layouts  5.22 us (5%)
    pallas_call x1, Pallas kernels, shards(): pl.pallas_call(kernel, out_shape=[jax.ShapeDtypeStruct(a.shape, BF16) for...  99.7 us
    unnamed x10, local copies, waits for them, and re-layouts  5.22 us

profile of v1, /device:TPU:1, one launch (start us, length us, event | category | flops | bytes accessed | tf_op | source)
XLA Modules:
  0.0 105.6 jit_solution(5717677895393745505)
XLA Ops:
  0.6 99.7 %shard_map.75 = (bf16[128,4096]{1,0:T(8,128)(2,1)}, bf16[128,4096]{1,0:T(8,128)(2,1)}, bf16[128,1024]{1,0:T(8,128)(2,1)}, bf16[128,1024]{1,0:T(8,128)(2,1)}) custom-call(bf16[128,4096]{1,0:T(8,128)(2,1)} %q_in.1, bf16[128,1024]{1,0:T(8,128)(2,1)} %k_in.1, bf16[128,1024]{1,0:T(8,128)(2,1)} %v_in.1, bf16[128,4096]{1,0:T(8,128)(2,1)} %do_in.1), custom_call_target="tpu_custom_call" | custom-call | tf_op jit(solution)/shard_map/pallas_call | solution.py:475
  100.4 0.0 copy-start
  100.4 2.4 %copy.12 = bf16[128,4096]{1,0:T(8,128)(2,1)} copy(bf16[128,4096]{1,0:T(8,128)(2,1)} %get-tuple-element.8) | data formatting | bytes 2097152
  102.8 0.0 copy-done
  102.8 0.0 copy-start.2
  102.8 1.0 copy.13
  103.7 0.1 copy-done.2
  103.8 0.0 copy-start.1
  103.8 0.7 copy.14
  104.6 0.3 copy-done.1
  104.9 0.7 copy.15
Async XLA Ops:
  100.4 2.4 %copy-start = (bf16[128,4096]{1,0:T(8,128)(2,1)S(1)}, bf16[128,4096]{1,0:T(8,128)(2,1)}, u32[]{:S(2)}) copy-start(bf16[128,4096]{1,0:T(8,128)(2,1)} %get-tuple-element.9) | copy-start | bytes 3145732
  102.8 1.1 %copy-start.2 = (bf16[128,1024]{1,0:T(8,128)(2,1)S(1)}, bf16[128,1024]{1,0:T(8,128)(2,1)}, u32[]{:S(2)}) copy-start(bf16[128,1024]{1,0:T(8,128)(2,1)} %get-tuple-element.10) | copy-start | bytes 786436
  103.8 1.0 copy-start.1

commit v2 on v1

--- a/solution.py
+++ b/solution.py
@@ -41,7 +41,7 @@
 
 def kernel(
     q_in, k_in, v_in, do_in, out_ref, gq_ref, gk_ref, gv_ref,
-    qb, dob, kv, kvt, probs, ob, gqb, db, stats, outb, gqout,
+    qb, dob, kv, kvt, probs, slopes, ob, gqb, db, stats, outb, gqout,
     xs, sumb, sg, rsz, rsy, rsx, acc1, acc2, acc3,
     dkv, own, gsend, grecv, fin,
     kv_send, kv_recv, q_send, do_send, q_recv, do_recv,
@@ -119,17 +119,13 @@
         for i, ref in enumerate((k_in, v_in)):
             send(
                 ref.at[:, pl.ds(al(half * GROUPS + g, D), D)],
-                kv.at[i, pl.ds(al(slot * 2 + core, ROWS), ROWS), pl.ds(g * D, D)],
+                kv.at[i, pl.ds(al(slot * 2 + core, ROWS), ROWS), pl.ds(al(g, D), D)],
                 kv_send.at[sem],
                 kv_recv.at[slot, g],
                 device,
             )
 
-    for g in range(GROUPS):
-        send_kv(g, 3, 1 - core, 0, sister)
-
-    for g in range(GROUPS):
-
+    def send_group(g):
         @pl.when(xh == 0)
         def _():
             for c in range(2):
@@ -137,17 +133,18 @@
 
         for h in range(4):
             send_kv(g, xh, h % 2, 3 + h, (after, h))
-        send(
-            q_in.at[:, pl.ds(al((1 - core) * GROUPS + g, REPEAT * D), REPEAT * D)],
-            qb.at[my_rows, pl.ds(g * REPEAT * D, REPEAT * D)],
-            q_send.at[g], q_recv.at[g], sister,
-        )
-    for g in range(GROUPS):
-        send(
-            do_in.at[:, pl.ds(al((1 - core) * GROUPS + g, REPEAT * D), REPEAT * D)],
-            dob.at[my_rows, pl.ds(g * REPEAT * D, REPEAT * D)],
-            do_send.at[g], do_recv.at[g], sister,
-        )
+
+    for g in range(GROUPS):
+        send_kv(g, 3, 1 - core, 0, sister)
+    send_group(0)
+    for ref, buf, send_sem, recv_sem in ((q_in, qb, q_send, q_recv), (do_in, dob, do_send, do_recv)):
+        for g in range(GROUPS):
+            send(
+                ref.at[:, pl.ds(al((1 - core) * GROUPS + g, REPEAT * D), REPEAT * D)],
+                buf.at[my_rows, pl.ds(g * REPEAT * D, REPEAT * D)],
+                send_sem.at[g], recv_sem.at[g], sister,
+            )
+    send_group(1)
 
     for g in range(GROUPS):
         wait(kv.at[:, pl.ds(3 * CHIP, CHIP), pl.ds(g * D, D)], kv_recv.at[3, g])
@@ -187,7 +184,7 @@
     causal = lax.broadcasted_iota(jnp.int32, (CHIP, CHIP), 0) <= lax.broadcasted_iota(jnp.int32, (CHIP, CHIP), 1)
 
     def band_forward(g):
-        group = pl.ds(g * D, D)
+        group = pl.ds(al(g, D), D)
         for slot in range(2):
             wait(kv.at[:, pl.ds(slot * CHIP, CHIP), group], kv_recv.at[slot, g])
 
@@ -195,14 +192,19 @@
         def _():
             wait(kv.at[:, pl.ds(2 * CHIP, CHIP), group], kv_recv.at[2, g])
 
-        wait(qb.at[:, pl.ds(g * REPEAT * D, REPEAT * D)], q_recv.at[g])
+        wait(qb.at[:, pl.ds(al(g, REPEAT * D), REPEAT * D)], q_recv.at[g])
+
+        @pl.when(g + 2 < GROUPS)
+        def _():
+            send_group(g + 2)
+
         for i in range(2):
-            kvt[i, g] = kv[i, :, g * D : (g + 1) * D].T
-
-        def one(j, carry):
-            h = g * REPEAT + j
-            q = qb[:, pl.ds(al(h, D), D)]
-            s = dot_t(kv[0, :, g * D : (g + 1) * D], q)
+            kvt[i, g] = kv[i, :, group].T
+
+        for j in range(REPEAT):
+            columns = slice(j * CHIP, (j + 1) * CHIP)
+            q = qb[:, pl.ds(al(g * REPEAT + j, D), D)]
+            s = dot_t(kv[0, :, group], q)
             s_before, s_partner = s[: 2 * CHIP], s[2 * CHIP : 3 * CHIP]
             s_own = jnp.where(causal, s[3 * CHIP :], LOWEST)
             top = jnp.maximum(
@@ -220,58 +222,53 @@
                 + jnp.sum(w_partner, axis=0, keepdims=True)
                 + jnp.sum(w_own, axis=0, keepdims=True)
             )
-            probs[h, : 2 * CHIP, :] = w_before.astype(BF16)
-            probs[h, 2 * CHIP : 3 * CHIP, :] = w_partner.astype(BF16)
-            probs[h, 3 * CHIP :, :] = w_own.astype(BF16)
-            ob[h] = dot(kvt[1, g], probs[h])
-            stats[h, 0:1, :] = top
-            stats[h, 1:2, :] = total
-            return carry
-
-        lax.fori_loop(0, REPEAT, one, 0)
-
-    seen = lax.broadcasted_iota(jnp.int32, (NCTX, CHIP), 0) < ctx
+            low = jnp.concatenate([w.astype(BF16) for w in (w_before, w_partner, w_own)], axis=0)
+            probs[g, :, columns] = low
+            ob[g, :, columns] = dot(kvt[1, g], low)
+            stats[g, 0:1, columns] = top
+            stats[g, 1:2, columns] = total
+
+    seen = lax.broadcasted_iota(jnp.int32, (NCTX, REPEAT * CHIP), 0) < ctx
+
+    def stacked_queries(g):
+        return jnp.concatenate([qb[:, pl.ds(al(g * REPEAT + j, D), D)] for j in range(REPEAT)], axis=0)
 
     def summary_part(g):
         sum_k = sumb[pl.ds(g, NCTX, stride=8), :]
         sum_v = sumb[pl.ds(GROUPS + g, NCTX, stride=8), :]
         sum_kt, sum_vt = sum_k.T.astype(BF16), sum_v.T.astype(BF16)
         sum_k, sum_v = sum_k.astype(BF16), sum_v.astype(BF16)
-        wait(dob.at[:, pl.ds(g * REPEAT * D, REPEAT * D)], do_recv.at[g])
-
-        def one(j, carry):
-            grad_k, grad_v = carry
-            h = g * REPEAT + j
-            cols = pl.ds(al(h, D), D)
-            q = qb[:, cols]
-            s = jnp.where(seen, dot_t(sum_k, q), LOWEST)
-            s_top = jnp.max(s, axis=0, keepdims=True) * LOG2
-            w = jnp.where(seen, jnp.exp2(s * LOG2 - s_top), 0.0)
-            b_top, b_total = stats[h, 0:1, :], stats[h, 1:2, :]
-            top = jnp.maximum(s_top, b_top)
-            b_part, s_part = jnp.exp2(b_top - top), jnp.exp2(s_top - top)
-            inverse = 1.0 / (b_part * b_total + s_part * jnp.sum(w, axis=0, keepdims=True))
-            b_part, s_part = b_part * inverse, s_part * inverse
-            w_low = w.astype(BF16)
-            attended = ob[h] * b_part + dot(sum_vt, w_low) * s_part
-            outb[:, cols] = attended.T.astype(BF16)
-            grad_out = dob[:, cols].astype(F32).T
-            b_grad = (grad_out * (16.0 * b_part)).astype(BF16)
-            s_grad = (grad_out * (16.0 * s_part)).astype(BF16)
-            db[h] = b_grad
-            stats[h, 2:3, :] = jnp.sum(b_grad.astype(F32) * attended, axis=0, keepdims=True)
-            s_dot = jnp.sum(s_grad.astype(F32) * attended, axis=0, keepdims=True)
-            slope = (w * (dot(sum_v, s_grad) - s_dot)).astype(BF16)
-            gqb[h] = dot(sum_kt, slope)
-            return grad_k + dot(slope, q), grad_v + dot_t(w_low, s_grad)
-
-        zero = jnp.zeros((NCTX, D), F32)
-        grad_k, grad_v = lax.fori_loop(0, REPEAT, one, (zero, zero))
-        sg[pl.ds(g, NCTX, stride=8), :] = grad_k * SCALE
-        sg[pl.ds(GROUPS + g, NCTX, stride=8), :] = grad_v
+        wait(dob.at[:, pl.ds(al(g, REPEAT * D), REPEAT * D)], do_recv.at[g])
+        q = stacked_queries(g)
+        s = jnp.where(seen, dot_t(sum_k, q), LOWEST)
+        s_top = jnp.max(s, axis=0, keepdims=True) * LOG2
+        w = jnp.where(seen, jnp.exp2(s * LOG2 - s_top), 0.0)
+        b_top, b_total = stats[g, 0:1, :], stats[g, 1:2, :]
+        top = jnp.maximum(s_top, b_top)
+        b_part, s_part = jnp.exp2(b_top - top), jnp.exp2(s_top - top)
+        inverse = 1.0 / (b_part * b_total + s_part * jnp.sum(w, axis=0, keepdims=True))
+        b_part, s_part = b_part * inverse, s_part * inverse
+        w_low = w.astype(BF16)
+        attended = ob[g] * b_part + dot(sum_vt, w_low) * s_part
+        grads = []
+        for j in range(REPEAT):
+            cols = pl.ds(al(g * REPEAT + j, D), D)
+            outb[:, cols] = attended[:, j * CHIP : (j + 1) * CHIP].T.astype(BF16)
+            grads.append(dob[:, cols].astype(F32).T)
+        grad_out = jnp.concatenate(grads, axis=1)
+        b_grad = (grad_out * (16.0 * b_part)).astype(BF16)
+        s_grad = (grad_out * (16.0 * s_part)).astype(BF16)
+        db[g] = b_grad
+        stats[g, 2:3, :] = jnp.sum(b_grad.astype(F32) * attended, axis=0, keepdims=True)
+        s_dot = jnp.sum(s_grad.astype(F32) * attended, axis=0, keepdims=True)
+        slope = (w * (dot(sum_v, s_grad) - s_dot)).astype(BF16)
+        gqb[g] = dot(sum_kt, slope)
+        sg[pl.ds(g, NCTX, stride=8), :] = dot(slope, q) * SCALE
+        sg[pl.ds(GROUPS + g, NCTX, stride=8), :] = dot_t(w_low, s_grad)
+        give(outb, out_ref, g, 0)
 
     def give(buf, ref, g, which):
-        cols = pl.ds(g * REPEAT * D, REPEAT * D)
+        cols = pl.ds(al(g, REPEAT * D), REPEAT * D)
         out_cols = pl.ds(al(core * GROUPS + g, REPEAT * D), REPEAT * D)
         send(buf.at[her_rows, cols], ref.at[:, out_cols], o_send.at[which, g], o_recv.at[which, g], sister)
         local(buf.at[my_rows, cols], ref.at[:, out_cols], o_local.at[which, g])
@@ -312,32 +309,17 @@
         acc3[...] = total / BLOCK
 
     def band_backward(g):
-        def one(j, carry):
-            h = g * REPEAT + j
-            cols = pl.ds(al(h, D), D)
-            q = qb[:, cols]
-            grad = db[h]
-            back = dot(kv[1, :, g * D : (g + 1) * D], grad)
-            low = probs[h]
-            slope = (low.astype(F32) * (back - stats[h, 2:3, :])).astype(BF16)
-            grad_q = (gqb[h] + dot(kvt[0, g], slope)) * SCALE
-            gqout[:, cols] = grad_q.T.astype(BF16)
-            grad_k = dot(slope, q)
-            grad_v = dot_t(low, grad)
-
-            @pl.when(j == 0)
-            def _():
-                dkv[0] = grad_k
-                dkv[1] = grad_v
-
-            @pl.when(j > 0)
-            def _():
-                dkv[0] += grad_k
-                dkv[1] += grad_v
-
-            return carry
-
-        lax.fori_loop(0, REPEAT, one, 0)
+        group = pl.ds(al(g, D), D)
+        for j in range(REPEAT):
+            columns = slice(j * CHIP, (j + 1) * CHIP)
+            back = dot(kv[1, :, group], db[g, :, columns])
+            slope = (probs[g, :, columns].astype(F32) * (back - stats[g, 2:3, columns])).astype(BF16)
+            slopes[:, columns] = slope
+            grad_q = (gqb[g, :, columns] + dot(kvt[0, g], slope)) * SCALE
+            gqout[:, pl.ds(al(g * REPEAT + j, D), D)] = grad_q.T.astype(BF16)
+        give(gqout, gq_ref, g, 1)
+        dkv[0] = dot(slopes[...], stacked_queries(g))
+        dkv[1] = dot_t(probs[g], db[g])
         own[0, g] = dkv[0, 3 * CHIP :, :] * SCALE
         own[1, g] = dkv[1, 3 * CHIP :, :]
         for slot in range(3):
@@ -370,28 +352,46 @@
             send(fin.at[g, i, her_rows, :], ref.at[:, cols], f_send.at[i, g], f_recv.at[i, g], sister)
             local(fin.at[g, i, my_rows, :], ref.at[:, cols], f_local.at[i, g])
 
-    band_forward(0)
     summaries_along_y()
-    band_forward(1)
-    summaries_along_z()
-    band_forward(2)
-    band_forward(3)
-    summaries_arrived()
-    for g in range(GROUPS):
-        summary_part(g)
-        give(outb, out_ref, g, 0)
-    grads_along_z()
-    band_backward(0)
-    give(gqout, gq_ref, 0, 1)
-    grads_along_y()
-    band_backward(1)
-    give(gqout, gq_ref, 1, 1)
+
+    def step(t, carry):
+        @pl.when(t < GROUPS)
+        def _():
+            band_forward(t)
+
+        @pl.when(t == 0)
+        def _():
+            summaries_along_z()
+
+        @pl.when(t == 1)
+        def _():
+            summaries_arrived()
+
+        @pl.when((t > 0) & (t < GROUPS))
+        def _():
+            def part(g, carry):
+                summary_part(g)
+                return carry
+
+            lax.fori_loop(jnp.where(t == 1, 0, t), t + 1, part, 0)
+
+        @pl.when(t == GROUPS - 1)
+        def _():
+            grads_along_z()
+
+        @pl.when(t == GROUPS)
+        def _():
+            grads_along_y()
+
+        @pl.when(t > 0)
+        def _():
+            band_backward(t - 1)
+
+        return carry
+
+    lax.fori_loop(0, GROUPS + 1, step, 0)
     grads_along_x()
-    band_backward(2)
-    give(gqout, gq_ref, 2, 1)
     grads_arrived()
-    band_backward(3)
-    give(gqout, gq_ref, 3, 1)
     for g in range(GROUPS):
         finish(g)
 
@@ -435,18 +435,18 @@
 
 
 def shards(queries, keys, values, cotangent):
-    heads = GROUPS * REPEAT
     dma = pltpu.SemaphoreType.DMA
     scratch = [
         pltpu.VMEM((CHIP, QCOLS), BF16),
         pltpu.VMEM((CHIP, QCOLS), BF16),
         pltpu.VMEM((2, BAND, KCOLS), BF16),
         pltpu.VMEM((2, GROUPS, D, BAND), BF16),
-        pltpu.VMEM((heads, BAND, CHIP), BF16),
-        pltpu.VMEM((heads, D, CHIP), F32),
-        pltpu.VMEM((heads, D, CHIP), F32),
-        pltpu.VMEM((heads, D, CHIP), BF16),
-        pltpu.VMEM((heads, 8, CHIP), F32),
+        pltpu.VMEM((GROUPS, BAND, REPEAT * CHIP), BF16),
+        pltpu.VMEM((BAND, REPEAT * CHIP), BF16),
+        pltpu.VMEM((GROUPS, D, REPEAT * CHIP), F32),
+        pltpu.VMEM((GROUPS, D, REPEAT * CHIP), F32),
+        pltpu.VMEM((GROUPS, D, REPEAT * CHIP), BF16),
+        pltpu.VMEM((GROUPS, 8, REPEAT * CHIP), F32),
         pltpu.VMEM((CHIP, QCOLS), BF16),
         pltpu.VMEM((CHIP, QCOLS), BF16),
         pltpu.VMEM((NX, 8, D), F32),

time: 107 us -> 86.5 us (0.81)
  Pallas kernels: 99.7 us -> 79.2 us
    pallas_call x1, Pallas kernels: 99.7 us -> 79.2 us  [shards(): pl.pallas_call(kernel, out_shape=[jax.ShapeDtypeStruct(a.shape, BF16) for...]
where the time goes in v2:
time: 86.5 us; the launch traced here: 85.1 us
  Pallas kernels  79.2 us (92%)
  local copies, waits for them, and re-layouts  5.22 us (6%)
    pallas_call x1, Pallas kernels, shards(): pl.pallas_call(kernel, out_shape=[jax.ShapeDtypeStruct(a.shape, BF16) for...  79.2 us
    unnamed x10, local copies, waits for them, and re-layouts  5.22 us

profile of v2, /device:TPU:1, one launch (start us, length us, event | category | flops | bytes accessed | tf_op | source)
XLA Modules:
  0.0 85.1 jit_solution(8871537353404119685)
XLA Ops:
  0.6 79.2 %shard_map.75 = (bf16[128,4096]{1,0:T(8,128)(2,1)}, bf16[128,4096]{1,0:T(8,128)(2,1)}, bf16[128,1024]{1,0:T(8,128)(2,1)}, bf16[128,1024]{1,0:T(8,128)(2,1)}) custom-call(bf16[128,4096]{1,0:T(8,128)(2,1)} %q_in.1, bf16[128,1024]{1,0:T(8,128)(2,1)} %k_in.1, bf16[128,1024]{1,0:T(8,128)(2,1)} %v_in.1, bf16[128,4096]{1,0:T(8,128)(2,1)} %do_in.1), custom_call_target="tpu_custom_call" | custom-call | tf_op jit(solution)/shard_map/pallas_call | solution.py:475
  79.9 0.0 copy-start
  79.9 2.4 %copy.12 = bf16[128,4096]{1,0:T(8,128)(2,1)} copy(bf16[128,4096]{1,0:T(8,128)(2,1)} %get-tuple-element.8) | data formatting | bytes 2097152
  82.3 0.0 copy-done
  82.3 0.0 copy-start.2
  82.3 1.0 %copy.13 = bf16[128,4096]{1,0:T(8,128)(2,1)} copy(bf16[128,4096]{1,0:T(8,128)(2,1)S(1)} %copy-done) | data formatting | bytes 2097152
  83.2 0.1 copy-done.2
  83.4 0.0 copy-start.1
  83.4 0.7 copy.14
  84.1 0.3 copy-done.1
  84.4 0.7 copy.15
Async XLA Ops:
  79.9 2.4 %copy-start = (bf16[128,4096]{1,0:T(8,128)(2,1)S(1)}, bf16[128,4096]{1,0:T(8,128)(2,1)}, u32[]{:S(2)}) copy-start(bf16[128,4096]{1,0:T(8,128)(2,1)} %get-tuple-element.9) | copy-start | bytes 3145732
  82.3 1.1 %copy-start.2 = (bf16[128,1024]{1,0:T(8,128)(2,1)S(1)}, bf16[128,1024]{1,0:T(8,128)(2,1)}, u32[]{:S(2)}) copy-start(bf16[128,1024]{1,0:T(8,128)(2,1)} %get-tuple-element.10) | copy-start | bytes 786436
  83.4 1.0 %copy-start.1 = (bf16[128,1024]{1,0:T(8,128)(2,1)S(1)}, bf16[128,1024]{1,0:T(8,128)(2,1)}, u32[]{:S(2)}) copy-start(bf16[128,1024]{1,0:T(8,128)(2,1)} %get-tuple-element.11) | copy-start | bytes 786436

commit v3 on v2

--- a/solution.py
+++ b/solution.py
@@ -42,9 +42,9 @@
 def kernel(
     q_in, k_in, v_in, do_in, out_ref, gq_ref, gk_ref, gv_ref,
     qb, dob, kv, kvt, probs, slopes, ob, gqb, db, stats, outb, gqout,
-    xs, sumb, sg, rsz, rsy, rsx, acc1, acc2, acc3,
-    dkv, own, gsend, grecv, fin,
-    kv_send, kv_recv, q_send, do_send, q_recv, do_recv,
+    kvl, stage, sums, xs, sumb, sg, rsz, rsy, rsx, acc1, acc2, acc3,
+    own, gsend, grecv, fin,
+    l_sem, st_send, st_recv, kv_send, kv_recv, own_recv, q_send, do_send, q_recv, do_recv,
     xs_send, xs_recv, ys_send, ys_recv, zs_send, zs_recv,
     rz_send, rz_recv, ry_send, ry_recv, rx_send, rx_recv,
     g_send, g_recv, o_send, o_recv, o_local, f_send, f_recv, f_local,
@@ -60,6 +60,8 @@
     sister = (ctx, xh * 2 + 1 - core)
     after = lax.rem(ctx + 1, NCTX)
     before = lax.rem(ctx + NCTX - 1, NCTX)
+    onward = lax.rem(ctx + 2, NCTX)
+    behind = lax.rem(ctx + NCTX - 2, NCTX)
 
     def at_x(d):
         other = lax.rem(x + d, NX)
@@ -87,80 +89,95 @@
     my_rows = pl.ds(al(core, ROWS), ROWS)
     her_rows = pl.ds(al(1 - core, ROWS), ROWS)
 
-    for g in range(GROUPS):
-        for i, ref in enumerate((k_in, v_in)):
-            local(
-                ref.at[:, pl.ds(al(core * GROUPS + g, D), D)],
-                kv.at[i, pl.ds(al(6 + core, ROWS), ROWS), pl.ds(g * D, D)],
-                kv_recv.at[3, g],
-            )
-    for g in range(GROUPS):
-        for ref, buf, sem in ((q_in, qb, q_recv), (do_in, dob, do_recv)):
-            local(
-                ref.at[:, pl.ds(al(core * GROUPS + g, REPEAT * D), REPEAT * D)],
-                buf.at[my_rows, pl.ds(g * REPEAT * D, REPEAT * D)],
-                sem.at[g],
-            )
-
-    @pl.when(xh == 0)
-    def _():
-        kv[:, 2 * CHIP : 3 * CHIP, :] = jnp.zeros((2, CHIP, KCOLS), BF16)
-
     barrier = pltpu.get_barrier_semaphore()
     partners = [sister]
     partners += [(ctx, (1 - xh) * 2 + c) for c in range(2)]
     partners += [(c, h) for c in (after, before) for h in range(4)]
+    partners += [(onward, head), (behind, head)]
     partners += [at_y(d)[1] for d in range(1, NY)] + [at_z(d)[1] for d in range(1, NZ)]
     for device in partners:
         pl.semaphore_signal(barrier, inc=1, device_id=device, device_id_type=MESH)
+
+    for i, ref in enumerate((k_in, v_in)):
+        local(ref, kvl.at[i], l_sem.at[i])
+
+    for i, ref in enumerate((k_in, v_in)):
+        local(ref.at[:, pl.ds(al(core, KCOLS), KCOLS)], kv.at[i, pl.ds(al(6 + core, ROWS), ROWS), :], own_recv)
+    for ref, buf, sem in ((q_in, qb, q_recv), (do_in, dob, do_recv)):
+        local(ref.at[:, pl.ds(al(core, QCOLS), QCOLS)], buf.at[my_rows, :], sem)
+
+    @pl.when(xh == 0)
+    def _():
+        kv[:, 2 * CHIP : 3 * CHIP, :] = jnp.zeros((2, CHIP, KCOLS), BF16)
+
+    pieces = ([], [])
+    for i in range(2):
+        wait(kvl.at[i], l_sem.at[i])
+        total = jnp.sum(kvl[i].astype(F32), axis=0, keepdims=True)
+        for half in range(2):
+            pieces[half].extend(total[:, (half * GROUPS + g) * D : (half * GROUPS + g + 1) * D] for g in range(GROUPS))
+    for half in range(2):
+        sums[half] = jnp.concatenate(pieces[half], axis=0)
+    xs[0] = sums[core]
     pl.semaphore_wait(barrier, len(partners))
-
-    def send_kv(g, slot, half, sem, device):
-        for i, ref in enumerate((k_in, v_in)):
-            send(
-                ref.at[:, pl.ds(al(half * GROUPS + g, D), D)],
-                kv.at[i, pl.ds(al(slot * 2 + core, ROWS), ROWS), pl.ds(al(g, D), D)],
-                kv_send.at[sem],
-                kv_recv.at[slot, g],
-                device,
-            )
+    for d in range(NX):
+        for other in range(2):
+            if d + other > 0:
+                half = 1 - core if other else core
+                ctx_x, head_x = at_x(d)[1]
+                slot = 2 * d + other
+                device = (ctx_x, head_x - core + half)
+                send(sums.at[half], xs.at[slot], xs_send.at[slot], xs_recv.at[slot], device)
+
+    def send_kv(src, g, slot, half, sem, device):
+        send(
+            src.at[:, :, pl.ds(al(half * GROUPS + g, D), D)],
+            kv.at[:, pl.ds(al(slot * 2 + core, ROWS), ROWS), pl.ds(al(g, D), D)],
+            kv_send.at[sem],
+            kv_recv.at[slot, g],
+            device,
+        )
+
+    def send_ahead(g):
+        @pl.when(xl == 1)
+        def _():
+            for half in range(2):
+                cols = pl.ds(al(half * GROUPS + g, D), D)
+                send(kvl.at[:, :, cols], stage.at[:, :, cols], st_send, st_recv.at[g], (onward, head))
 
     def send_group(g):
+        @pl.when(xl == 0)
+        def _():
+            for h in range(4):
+                send_kv(kvl, g, xh, h % 2, 3 + h, (after, h))
+
         @pl.when(xh == 0)
         def _():
             for c in range(2):
-                send_kv(g, 2, c, 1 + c, (ctx, 2 + c))
-
-        for h in range(4):
-            send_kv(g, xh, h % 2, 3 + h, (after, h))
-
-    for g in range(GROUPS):
-        send_kv(g, 3, 1 - core, 0, sister)
-    send_group(0)
-    for ref, buf, send_sem, recv_sem in ((q_in, qb, q_send, q_recv), (do_in, dob, do_send, do_recv)):
-        for g in range(GROUPS):
-            send(
-                ref.at[:, pl.ds(al((1 - core) * GROUPS + g, REPEAT * D), REPEAT * D)],
-                buf.at[my_rows, pl.ds(g * REPEAT * D, REPEAT * D)],
-                send_sem.at[g], recv_sem.at[g], sister,
-            )
-    send_group(1)
-
-    for g in range(GROUPS):
-        wait(kv.at[:, pl.ds(3 * CHIP, CHIP), pl.ds(g * D, D)], kv_recv.at[3, g])
-    pieces = []
-    for i in range(2):
-        total = jnp.sum(kv[i, 3 * CHIP :, :].astype(F32), axis=0, keepdims=True)
-        pieces += [total[:, g * D : (g + 1) * D] for g in range(GROUPS)]
-    xs[0] = jnp.concatenate(pieces, axis=0)
-    for d in range(1, NX):
-        send(xs.at[0], xs.at[d], xs_send.at[d], xs_recv.at[d], at_x(d)[1])
+                send_kv(kvl, g, 2, c, 1 + c, (ctx, 2 + c))
+
+    def pass_on(g):
+        @pl.when(xl == 1)
+        def _():
+            wait(stage.at[:, :, pl.ds(0, 2 * D)], st_recv.at[g])
+            for h in range(4):
+                send_kv(stage, g, xh, h % 2, 3 + h, (before, h))
+
+    def exchange_cores():
+        send(
+            kvl.at[:, :, pl.ds(al(1 - core, KCOLS), KCOLS)],
+            kv.at[:, pl.ds(al(6 + core, ROWS), ROWS), :],
+            kv_send.at[0], own_recv, sister,
+        )
+        her_cols = pl.ds(al(1 - core, QCOLS), QCOLS)
+        send(q_in.at[:, her_cols], qb.at[my_rows, :], q_send, q_recv, sister)
+        send(do_in.at[:, her_cols], dob.at[my_rows, :], do_send, do_recv, sister)
 
     def summaries_along_y():
-        for d in range(1, NX):
-            wait(xs.at[d], xs_recv.at[d])
-        mine = (xs[0] + xs[2]) / BLOCK
-        others = (xs[1] + xs[3]) / BLOCK
+        for slot in range(1, 2 * NX):
+            wait(xs.at[slot], xs_recv.at[slot])
+        mine = (xs[0] + xs[1] + xs[4] + xs[5]) / BLOCK
+        others = (xs[2] + xs[3] + xs[6] + xs[7]) / BLOCK
         first = z * (2 * NY) + y * 2
         sumb[pl.ds(al(first + xl, 8), 8), :] = mine.astype(BF16).astype(F32)
         sumb[pl.ds(al(first + 1 - xl, 8), 8), :] = others.astype(BF16).astype(F32)
@@ -185,6 +202,11 @@
 
     def band_forward(g):
         group = pl.ds(al(g, D), D)
+        @pl.when(g == 0)
+        def _():
+            wait(kv.at[:, pl.ds(3 * CHIP, CHIP), :], own_recv)
+            wait(qb, q_recv)
+
         for slot in range(2):
             wait(kv.at[:, pl.ds(slot * CHIP, CHIP), group], kv_recv.at[slot, g])
 
@@ -192,11 +214,14 @@
         def _():
             wait(kv.at[:, pl.ds(2 * CHIP, CHIP), group], kv_recv.at[2, g])
 
-        wait(qb.at[:, pl.ds(al(g, REPEAT * D), REPEAT * D)], q_recv.at[g])
+        @pl.when(g + 1 < GROUPS)
+        def _():
+            send_group(g + 1)
+            pass_on(g + 1)
 
         @pl.when(g + 2 < GROUPS)
         def _():
-            send_group(g + 2)
+            send_ahead(g + 2)
 
         for i in range(2):
             kvt[i, g] = kv[i, :, group].T
@@ -238,7 +263,6 @@
         sum_v = sumb[pl.ds(GROUPS + g, NCTX, stride=8), :]
         sum_kt, sum_vt = sum_k.T.astype(BF16), sum_v.T.astype(BF16)
         sum_k, sum_v = sum_k.astype(BF16), sum_v.astype(BF16)
-        wait(dob.at[:, pl.ds(al(g, REPEAT * D), REPEAT * D)], do_recv.at[g])
         q = stacked_queries(g)
         s = jnp.where(seen, dot_t(sum_k, q), LOWEST)
         s_top = jnp.max(s, axis=0, keepdims=True) * LOG2
@@ -315,16 +339,22 @@
             back = dot(kv[1, :, group], db[g, :, columns])
             slope = (probs[g, :, columns].astype(F32) * (back - stats[g, 2:3, columns])).astype(BF16)
             slopes[:, columns] = slope
-            grad_q = (gqb[g, :, columns] + dot(kvt[0, g], slope)) * SCALE
-            gqout[:, pl.ds(al(g * REPEAT + j, D), D)] = grad_q.T.astype(BF16)
-        give(gqout, gq_ref, g, 1)
-        dkv[0] = dot(slopes[...], stacked_queries(g))
-        dkv[1] = dot_t(probs[g], db[g])
-        own[0, g] = dkv[0, 3 * CHIP :, :] * SCALE
-        own[1, g] = dkv[1, 3 * CHIP :, :]
+
+        @pl.when(g == GROUPS - 2)
+        def _():
+            grads_along_y()
+
+        @pl.when(g == GROUPS - 1)
+        def _():
+            grads_along_x()
+
+        q = stacked_queries(g)
+        others = 3 * CHIP
+        grad_k = (dot(slopes[:others, :], q) * SCALE).astype(BF16)
+        grad_v = dot_t(probs[g, :others, :], db[g]).astype(BF16)
         for slot in range(3):
-            gsend[slot, g, 0] = (dkv[0, slot * CHIP : (slot + 1) * CHIP, :] * SCALE).astype(BF16)
-            gsend[slot, g, 1] = dkv[1, slot * CHIP : (slot + 1) * CHIP, :].astype(BF16)
+            gsend[slot, g, 0] = grad_k[slot * CHIP : (slot + 1) * CHIP, :]
+            gsend[slot, g, 1] = grad_v[slot * CHIP : (slot + 1) * CHIP, :]
         for slot in range(2):
             send(
                 gsend.at[slot, g], grecv.at[xh, g], g_send.at[slot, g], g_recv.at[xh, g], (before, slot * 2 + core)
@@ -333,6 +363,13 @@
         @pl.when(xh == 1)
         def _():
             send(gsend.at[2, g], grecv.at[2, g], g_send.at[2, g], g_recv.at[2, g], (ctx, core))
+
+        own[0, g] = dot(slopes[others:, :], q) * SCALE
+        own[1, g] = dot_t(probs[g, others:, :], db[g])
+        grad_q = (gqb[g] + dot(kvt[0, g], slopes[...])) * SCALE
+        for j in range(REPEAT):
+            gqout[:, pl.ds(al(g * REPEAT + j, D), D)] = grad_q[:, j * CHIP : (j + 1) * CHIP].T.astype(BF16)
+        give(gqout, gq_ref, g, 1)
 
     def finish(g):
         for slot in range(2):
@@ -352,7 +389,13 @@
             send(fin.at[g, i, her_rows, :], ref.at[:, cols], f_send.at[i, g], f_recv.at[i, g], sister)
             local(fin.at[g, i, my_rows, :], ref.at[:, cols], f_local.at[i, g])
 
+    send_ahead(0)
+    send_group(0)
+    send_ahead(1)
+    exchange_cores()
     summaries_along_y()
+    pass_on(0)
+    summaries_along_z()
 
     def step(t, carry):
         @pl.when(t < GROUPS)
@@ -361,42 +404,37 @@
 
         @pl.when(t == 0)
         def _():
-            summaries_along_z()
-
-        @pl.when(t == 1)
-        def _():
             summaries_arrived()
-
-        @pl.when((t > 0) & (t < GROUPS))
-        def _():
-            def part(g, carry):
-                summary_part(g)
-                return carry
-
-            lax.fori_loop(jnp.where(t == 1, 0, t), t + 1, part, 0)
+            wait(dob, do_recv)
+
+        @pl.when(t < GROUPS)
+        def _():
+            summary_part(t)
 
         @pl.when(t == GROUPS - 1)
         def _():
             grads_along_z()
 
-        @pl.when(t == GROUPS)
-        def _():
-            grads_along_y()
-
-        @pl.when(t > 0)
-        def _():
-            band_backward(t - 1)
+        @pl.when(t != GROUPS - 2)
+        def _():
+            band_backward(t - lax.div(t, GROUPS - 1))
 
         return carry
 
     lax.fori_loop(0, GROUPS + 1, step, 0)
-    grads_along_x()
     grads_arrived()
     for g in range(GROUPS):
         finish(g)
 
     rows_all = kv.at[:, pl.ds(0, ROWS), :]
     wait(rows_all, kv_send.at[0])
+    wait(qb.at[my_rows, :], q_send)
+
+    @pl.when(xl == 1)
+    def _():
+        wait(kvl, st_send)
+
+    wait(dob.at[my_rows, :], do_send)
     for h in range(4):
         wait(rows_all, kv_send.at[3 + h])
 
@@ -412,8 +450,6 @@
 
     part = qb.at[my_rows, pl.ds(0, REPEAT * D)]
     for g in range(GROUPS):
-        wait(part, q_send.at[g])
-        wait(part, do_send.at[g])
         for slot in range(2):
             wait(gsend.at[slot, g], g_send.at[slot, g])
         for i in range(2):
@@ -424,14 +460,28 @@
             wait(fin.at[g, i, my_rows, :], f_recv.at[i, g])
             wait(fin.at[g, i, my_rows, :], f_local.at[i, g])
     for d in range(1, NX):
-        wait(xs.at[d], xs_send.at[d])
         wait(rsx.at[d], rx_send.at[d])
+    for slot in range(1, 2 * NX):
+        wait(xs.at[slot], xs_send.at[slot])
     for d in range(1, NY):
         wait(rsy.at[d], ys_send.at[d])
         wait(rsy.at[d], ry_send.at[d])
     for d in range(1, NZ):
         wait(rsz.at[d], zs_send.at[d])
         wait(rsz.at[d], rz_send.at[d])
+
+
+def deliver(*refs):
+    sources, targets, held, fetched, stored = refs[:4], refs[4:8], refs[8:12], refs[12], refs[13]
+    fetches = [pltpu.make_async_copy(sources[i], held[i], fetched.at[i]) for i in range(4)]
+    stores = [pltpu.make_async_copy(held[i], targets[i], stored.at[i]) for i in range(4)]
+    for copy in fetches:
+        copy.start()
+    for fetch, store in zip(fetches, stores):
+        fetch.wait()
+        store.start()
+    for store in stores:
+        store.wait()
 
 
 def shards(queries, keys, values, cotangent):
@@ -449,7 +499,10 @@
         pltpu.VMEM((GROUPS, 8, REPEAT * CHIP), F32),
         pltpu.VMEM((CHIP, QCOLS), BF16),
         pltpu.VMEM((CHIP, QCOLS), BF16),
-        pltpu.VMEM((NX, 8, D), F32),
+        pltpu.VMEM((2, ROWS, 2 * KCOLS), BF16),
+        pltpu.VMEM((2, ROWS, 2 * KCOLS), BF16),
+        pltpu.VMEM((2, 8, D), F32),
+        pltpu.VMEM((2 * NX, 8, D), F32),
         pltpu.VMEM((NCTX * 8, D), F32),
         pltpu.VMEM((NCTX * 8, D), F32),
         pltpu.VMEM((NZ, 64, D), F32),
@@ -458,21 +511,20 @@
         pltpu.VMEM((64, D), F32),
         pltpu.VMEM((16, D), F32),
         pltpu.VMEM((8, D), F32),
-        pltpu.VMEM((2, BAND, D), F32),
         pltpu.VMEM((2, GROUPS, CHIP, D), F32),
         pltpu.VMEM((3, GROUPS, 2, CHIP, D), BF16),
         pltpu.VMEM((3, GROUPS, 2, CHIP, D), BF16),
         pltpu.VMEM((GROUPS, 2, CHIP, D), BF16),
-        dma((7,)), dma((4, GROUPS)),
-        dma((GROUPS,)), dma((GROUPS,)), dma((GROUPS,)), dma((GROUPS,)),
-        dma((NX,)), dma((NX,)), dma((NY,)), dma((NY,)), dma((NZ,)), dma((NZ,)),
+        dma((2,)), dma, dma((GROUPS,)), dma((7,)), dma((4, GROUPS)),
+        dma, dma, dma, dma, dma,
+        dma((2 * NX,)), dma((2 * NX,)), dma((NY,)), dma((NY,)), dma((NZ,)), dma((NZ,)),
         dma((NZ,)), dma((NZ,)), dma((NY,)), dma((NY,)), dma((NX,)), dma((NX,)),
         dma((3, GROUPS)), dma((3, GROUPS)),
         dma((2, GROUPS)), dma((2, GROUPS)), dma((2, GROUPS)),
         dma((2, GROUPS)), dma((2, GROUPS)), dma((2, GROUPS)),
     ]
     anywhere = pl.BlockSpec(memory_space=pl.ANY)
-    return pl.pallas_call(
+    results = pl.pallas_call(
         kernel,
         out_shape=[jax.ShapeDtypeStruct(a.shape, BF16) for a in (queries, cotangent, keys, values)],
         in_specs=[anywhere] * 4,
@@ -482,6 +534,13 @@
             collective_id=0, has_side_effects=True, vmem_limit_bytes=56 * 1024 * 1024
         ),
     )(queries, keys, values, cotangent)
+    return pl.pallas_call(
+        deliver,
+        out_shape=[jax.ShapeDtypeStruct(a.shape, BF16) for a in results],
+        in_specs=[anywhere] * 4,
+        out_specs=[anywhere] * 4,
+        scratch_shapes=[pltpu.VMEM(a.shape, BF16) for a in results] + [dma((4,)), dma((4,))],
+    )(*results)
 
 
 def solution(mesh):

time: 86.5 us -> 83.2 us (0.962)
  the two profiles are of different devices: /device:TPU:1 before, /device:TPU:73 now
where the time goes in v3:
time: 83.2 us; the launch traced here: 83.1 us
  Pallas kernels  82.4 us (99%)
    pallas_call x1, Pallas kernels, shards(): pl.pallas_call(kernel, out_shape=[jax.ShapeDtypeStruct(a.shape, BF16) for...  79.7 us
    pallas_call x1, Pallas kernels, shards(): pl.pallas_call(deliver, out_shape=[jax.ShapeDtypeStruct(a.shape, BF16) fo...  2.77 us

profile of v3, /device:TPU:73, one launch (start us, length us, event | category | flops | bytes accessed | tf_op | source)
XLA Modules:
  0.0 83.1 jit_solution(16735369792490654229)
XLA Ops:
  0.6 79.7 %shard_map.75 = (bf16[128,4096]{1,0:T(8,128)(2,1)}, bf16[128,4096]{1,0:T(8,128)(2,1)}, bf16[128,1024]{1,0:T(8,128)(2,1)}, bf16[128,1024]{1,0:T(8,128)(2,1)}) custom-call(bf16[128,4096]{1,0:T(8,128)(2,1)} %q_in.1, bf16[128,1024]{1,0:T(8,128)(2,1)} %k_in.1, bf16[128,1024]{1,0:T(8,128)(2,1)} %v_in.1, bf16[128,4096]{1,0:T(8,128)(2,1)} %do_in.1), custom_call_target="tpu_custom_call" | custom-call | tf_op jit(solution)/shard_map/pallas_call | solution.py:527
  80.3 2.8 %shard_map.76 = (bf16[128,4096]{1,0:T(8,128)(2,1)}, bf16[128,4096]{1,0:T(8,128)(2,1)}, bf16[128,1024]{1,0:T(8,128)(2,1)}, bf16[128,1024]{1,0:T(8,128)(2,1)}) custom-call(bf16[128,4096]{1,0:T(8,128)(2,1)} %get-tuple-element.8.refs_0_, bf16[128,4096]{1,0:T(8,128)(2,1)} %get-tuple-element.9.refs_1_, bf16[128,1024]{1,0:T(8,128)(2,1)} %get-tuple-element.10.refs_2_, ...), custom_call_target="tpu_custom_call" | custom-call | tf_op jit(solution)/shard_map/pallas_call | solution.py:537

commit v4 on v3

--- a/solution.py
+++ b/solution.py
@@ -42,7 +42,7 @@
 def kernel(
     q_in, k_in, v_in, do_in, out_ref, gq_ref, gk_ref, gv_ref,
     qb, dob, kv, kvt, probs, slopes, ob, gqb, db, stats, outb, gqout,
-    kvl, stage, sums, xs, sumb, sg, rsz, rsy, rsx, acc1, acc2, acc3,
+    kvl, stage, sums, xs, sumb, sg, low, summary, sglow, rsz, rsy, rsx, acc1, acc2, acc3,
     own, gsend, grecv, fin,
     l_sem, st_send, st_recv, kv_send, kv_recv, own_recv, q_send, do_send, q_recv, do_recv,
     xs_send, xs_recv, ys_send, ys_recv, zs_send, zs_recv,
@@ -189,12 +189,14 @@
         for d in range(1, NY):
             wait(sumb.at[pl.ds(0, 16), :], ys_recv.at[d])
         rows = pl.ds(al(z, 64), 64)
+        low[rows, :] = sumb[rows, :].astype(BF16)
         for d in range(1, NZ):
-            send(sumb.at[rows, :], sumb.at[rows, :], zs_send.at[d], zs_recv.at[d], at_z(d)[1])
+            send(low.at[rows, :], low.at[rows, :], zs_send.at[d], zs_recv.at[d], at_z(d)[1])
 
     def summaries_arrived():
         for d in range(1, NZ):
-            wait(sumb.at[pl.ds(0, 64), :], zs_recv.at[d])
+            wait(low.at[pl.ds(0, 64), :], zs_recv.at[d])
+        summary[...] = low[...].astype(F32)
 
     no_before = jnp.where(ctx == 0, LOWEST, 0.0).astype(F32)
     no_partner = jnp.where(xh == 0, LOWEST, 0.0).astype(F32)
@@ -259,8 +261,8 @@
         return jnp.concatenate([qb[:, pl.ds(al(g * REPEAT + j, D), D)] for j in range(REPEAT)], axis=0)
 
     def summary_part(g):
-        sum_k = sumb[pl.ds(g, NCTX, stride=8), :]
-        sum_v = sumb[pl.ds(GROUPS + g, NCTX, stride=8), :]
+        sum_k = summary[pl.ds(g, NCTX, stride=8), :]
+        sum_v = summary[pl.ds(GROUPS + g, NCTX, stride=8), :]
         sum_kt, sum_vt = sum_k.T.astype(BF16), sum_v.T.astype(BF16)
         sum_k, sum_v = sum_k.astype(BF16), sum_v.astype(BF16)
         q = stacked_queries(g)
@@ -298,16 +300,17 @@
         local(buf.at[my_rows, cols], ref.at[:, out_cols], o_local.at[which, g])
 
     def grads_along_z():
+        sglow[...] = sg[...].astype(BF16)
         for d in range(1, NZ):
             other, device = at_z(d)
-            send(sg.at[pl.ds(al(other, 64), 64), :], rsz.at[d], rz_send.at[d], rz_recv.at[d], device)
+            send(sglow.at[pl.ds(al(other, 64), 64), :], rsz.at[d], rz_send.at[d], rz_recv.at[d], device)
 
     def grads_along_y():
         for d in range(1, NZ):
             wait(rsz.at[d], rz_recv.at[d])
         total = sg[pl.ds(al(z, 64), 64), :]
         for d in range(1, NZ):
-            total = total + rsz[d]
+            total = total + rsz[d].astype(F32)
         acc1[...] = total
         for d in range(1, NY):
             other, device = at_y(d)
@@ -391,9 +394,9 @@
 
     send_ahead(0)
     send_group(0)
-    send_ahead(1)
     exchange_cores()
     summaries_along_y()
+    send_ahead(1)
     pass_on(0)
     summaries_along_z()
 
@@ -505,7 +508,10 @@
         pltpu.VMEM((2 * NX, 8, D), F32),
         pltpu.VMEM((NCTX * 8, D), F32),
         pltpu.VMEM((NCTX * 8, D), F32),
-        pltpu.VMEM((NZ, 64, D), F32),
+        pltpu.VMEM((NCTX * 8, D), BF16),
+        pltpu.VMEM((NCTX * 8, D), F32),
+        pltpu.VMEM((NCTX * 8, D), BF16),
+        pltpu.VMEM((NZ, 64, D), BF16),
         pltpu.VMEM((NY, 16, D), F32),
         pltpu.VMEM((NX, 8, D), F32),
         pltpu.VMEM((64, D), F32),

time: 83.2 us -> 80.3 us (0.965)
  the two profiles are of different devices: /device:TPU:73 before, /device:TPU:1 now
where the time goes in v4:
time: 80.3 us; the launch traced here: 80.2 us
  Pallas kernels  79.5 us (99%)
    pallas_call x1, Pallas kernels, shards(): pl.pallas_call(kernel, out_shape=[jax.ShapeDtypeStruct(a.shape, BF16) for...  76.7 us
    pallas_call x1, Pallas kernels, shards(): pl.pallas_call(deliver, out_shape=[jax.ShapeDtypeStruct(a.shape, BF16) fo...  2.77 us

profile of v4, /device:TPU:1, one launch (start us, length us, event | category | flops | bytes accessed | tf_op | source)
XLA Modules:
  0.0 80.2 jit_solution(15574761225233453522)
XLA Ops:
  0.6 76.7 %shard_map.75 = (bf16[128,4096]{1,0:T(8,128)(2,1)}, bf16[128,4096]{1,0:T(8,128)(2,1)}, bf16[128,1024]{1,0:T(8,128)(2,1)}, bf16[128,1024]{1,0:T(8,128)(2,1)}) custom-call(bf16[128,4096]{1,0:T(8,128)(2,1)} %q_in.1, bf16[128,1024]{1,0:T(8,128)(2,1)} %k_in.1, bf16[128,1024]{1,0:T(8,128)(2,1)} %v_in.1, bf16[128,4096]{1,0:T(8,128)(2,1)} %do_in.1), custom_call_target="tpu_custom_call" | custom-call | tf_op jit(solution)/shard_map/pallas_call | solution.py:533
  77.4 2.8 %shard_map.76 = (bf16[128,4096]{1,0:T(8,128)(2,1)}, bf16[128,4096]{1,0:T(8,128)(2,1)}, bf16[128,1024]{1,0:T(8,128)(2,1)}, bf16[128,1024]{1,0:T(8,128)(2,1)}) custom-call(bf16[128,4096]{1,0:T(8,128)(2,1)} %get-tuple-element.8.refs_0_, bf16[128,4096]{1,0:T(8,128)(2,1)} %get-tuple-element.9.refs_1_, bf16[128,1024]{1,0:T(8,128)(2,1)} %get-tuple-element.10.refs_2_, ...), custom_call_target="tpu_custom_call" | custom-call | tf_op jit(solution)/shard_map/pallas_call | solution.py:543
